TPU v7x, 512 devices: a whole 4x4x16 slice. The times are simulated.
512 devices in a mesh: grp: 2 (over z_hi), seq: 8 (over y, core), hid: 32 (over x, z_lo).
Axes of the slice: x: 4, y: 4, z: 16 (z_hi: 2, z_lo: 8; z = z_hi * 8 + z_lo), core: 2. Of those that a mesh axis runs over, the one named last changes fastest.
Arguments:
- queries: bfloat16 [64, 4, 64, 576], P(('grp', 'hid')), may hold values from -25 to 25
- new_latents: bfloat16 [64, 4, 576], P(('grp', 'hid')), may hold values from -4 to 4
- latent_cache: bfloat16 [64, 2048, 576], P(('grp', 'hid'), 'seq'), may hold values from -4 to 4
- lengths: int32 [64], P(('grp', 'hid')), may hold values from 1 to 2048, 65536 in all
- positions: int32 [64], P(('grp', 'hid')), may hold values from 0 to 32767
- value_up: bfloat16 [64, 512, 128], P(('grp', 'hid')), may hold values from -0.8984375 to 0.8984375
- output_weight: bfloat16 [8192, 8192], P(('grp', 'hid'), 'seq'), may hold values from -0.0625 to 0.0625
- residual: bfloat16 [256, 8192], P(None, 'seq'), may hold values from -64 to 64
- norm_gain: float32 [8192], P('seq'), may hold values from 0.1 to 1.9
- gate_weight: bfloat16 [8192, 16384], P('seq', ('grp', 'hid')), may hold values from -0.0625 to 0.0625
- up_weight: bfloat16 [8192, 16384], P('seq', ('grp', 'hid')), may hold values from -0.0625 to 0.0625
- down_weight: bfloat16 [16384, 8192], P(('grp', 'hid'), 'seq'), may hold values from -0.046875 to 0.046875
Outputs:
- layer_out: bfloat16 [256, 8192], P(('grp', 'hid'), 'seq')
Inputs may be any that keep to these rules, and one draw needn't show every extreme that they name: `lengths`: some row holds exactly 2048 cached tokens.
All inputs are finite; a program needn't handle non-finite values. No bound on the sum of `lengths` on one device may be relied on, other than what follows from the above.
Results may differ from a plain program's by a relative error of at most 0.022.
Values may be sent and summed in bfloat16 or wider, within the bound.
A program may use at most 64 MiB of HBM per device.

v0:
```python
import math

import jax
import jax.numpy as jnp
from jax import lax
from jax.sharding import PartitionSpec as P

D = 8192
LATENT = 512


score_scale = 192.0 ** (-0.5)


def joined(part, axis, combine):
    gathered = jax.tree.map(lambda a: lax.all_gather(a, axis), part)

    def take(source):
        return jax.tree.map(lambda a: lax.dynamic_index_in_dim(a, source, 0, False), gathered)

    return lax.fori_loop(
        1, lax.axis_size(axis), lambda source, state: combine(state, take(source)), take(0)
    )


def rope_tables(positions, count, halfwidth):
    counter = jnp.arange(halfwidth, dtype=jnp.float32)
    frequency = jnp.exp(counter * (-math.log(1000000.0) / halfwidth))
    places = positions.astype(jnp.float32)[:, None] + jnp.arange(count, dtype=jnp.float32)[None, :]
    angles = places[:, :, None] * frequency
    return (jnp.cos(angles), jnp.sin(angles))


def rotate(vector, cosines, sines):
    halfwidth = cosines.shape[-1]
    leading = vector[..., :halfwidth]
    trailing = vector[..., halfwidth:]
    return jnp.concatenate(
        [leading * cosines - trailing * sines, trailing * cosines + leading * sines], axis=-1
    )


def full_inputs(queries, new_latents, positions):
    latent_width = LATENT
    halfwidth = (queries.shape[-1] - latent_width) // 2
    cosines, sines = rope_tables(positions, queries.shape[1], halfwidth)
    query_rope = rotate(
        queries[..., latent_width:].astype(jnp.float32),
        cosines[:, :, None, :],
        sines[:, :, None, :],
    )
    full_queries = jnp.concatenate(
        [queries[..., :latent_width], query_rope.astype(jnp.bfloat16)], axis=-1
    )
    key_rope = rotate(new_latents[..., latent_width:].astype(jnp.float32), cosines, sines)
    new_keys = jnp.concatenate(
        [new_latents[..., :latent_width], key_rope.astype(jnp.bfloat16)], axis=-1
    )
    return (full_queries, new_keys)


def combine_parts(earlier, latter):
    maxima = jnp.maximum(earlier[0], latter[0])
    factor_one = jnp.exp(earlier[0] - maxima)
    factor_two = jnp.exp(latter[0] - maxima)
    totals = earlier[1] * factor_one + latter[1] * factor_two
    mixture = earlier[2] * factor_one[..., None] + latter[2] * factor_two[..., None]
    return (maxima, totals, mixture)


def body(
    queries,
    new_latents,
    latent_cache,
    lengths,
    positions,
    value_up,
    output_weight,
    residual,
    norm_gain,
    gate_weight,
    up_weight,
    down_weight,
):
    full_queries, new_keys = full_inputs(queries, new_latents, positions)
    ctx_block = latent_cache.shape[1]
    offset = lax.axis_index("seq") * ctx_block
    places = offset + jnp.arange(ctx_block, dtype=jnp.int32)
    usable = (places[None, :] < lengths[:, None])[:, None, None, :]
    scores = (
        jnp.einsum("rthc,rjc->rthj", full_queries, latent_cache, preferred_element_type=jnp.float32)
        * score_scale
    )
    maxima = jnp.max(jnp.where(usable, scores, -1e30), axis=-1)
    weights = jnp.where(usable, jnp.exp(scores - maxima[..., None]), 0.0)
    totals = jnp.sum(weights, axis=-1)
    mixture = jnp.einsum(
        "rthj,rjc->rthc",
        weights.astype(jnp.bfloat16),
        latent_cache,
        preferred_element_type=jnp.float32,
    )[..., :LATENT]
    merged = joined((maxima, totals, mixture), "seq", combine_parts)
    new_count = full_queries.shape[1]
    nearby = (
        jnp.einsum("rthc,ruc->rthu", full_queries, new_keys, preferred_element_type=jnp.float32)
        * score_scale
    )
    causal = (jnp.arange(new_count)[None, :] <= jnp.arange(new_count)[:, None])[None, :, None, :]
    near_max = jnp.max(jnp.where(causal, nearby, -1e30), axis=-1)
    near_weights = jnp.where(causal, jnp.exp(nearby - near_max[..., None]), 0.0)
    near_totals = jnp.sum(near_weights, axis=-1)
    near_mixture = jnp.einsum(
        "rthu,ruc->rthc",
        near_weights.astype(jnp.bfloat16),
        new_keys[..., :LATENT],
        preferred_element_type=jnp.float32,
    )
    maxima, totals, mixture = combine_parts(merged, (near_max, near_totals, near_mixture))
    head_out = (mixture / totals[..., None]).astype(jnp.bfloat16)
    projected = jnp.einsum(
        "rthc,hcv->rthv",
        lax.all_to_all(head_out, ("grp", "hid"), split_axis=2, concat_axis=0, tiled=True),
        value_up,
        preferred_element_type=jnp.float32,
    ).astype(jnp.bfloat16)
    values = projected.reshape(projected.shape[0], projected.shape[1], -1)
    tokens = values.shape[0] * values.shape[1]
    flattened = values.reshape(tokens, -1)
    devices = lax.axis_size(("grp", "hid"))
    tok_block = tokens // devices
    row_start = lax.axis_index(("grp", "hid")) * tok_block
    attention = lax.psum(
        jnp.dot(flattened, output_weight, preferred_element_type=jnp.float32), ("grp", "hid")
    )
    stream = residual.astype(jnp.float32) + attention
    scaled = (stream * norm_gain).astype(jnp.bfloat16)
    squares = jnp.sum(stream * stream, axis=1)
    gate_part = jnp.dot(scaled, gate_weight, preferred_element_type=jnp.float32)
    up_part = jnp.dot(scaled, up_weight, preferred_element_type=jnp.float32)
    own_rows = lax.dynamic_slice_in_dim(stream, row_start, tok_block, 0)
    gate_sum, up_sum, square_sum = (
        lax.psum(gate_part.astype(jnp.bfloat16), "seq").astype(jnp.float32),
        lax.psum(up_part.astype(jnp.bfloat16), "seq").astype(jnp.float32),
        lax.psum(squares.astype(jnp.bfloat16), "seq").astype(jnp.float32),
    )
    inverse_rms = lax.rsqrt(square_sum / D + 1e-06)[:, None]
    hidden = (jax.nn.silu(gate_sum * inverse_rms) * (up_sum * inverse_rms)).astype(jnp.bfloat16)
    ffn_out = lax.psum_scatter(
        jnp.dot(hidden, down_weight, preferred_element_type=jnp.float32),
        ("grp", "hid"),
        scatter_dimension=0,
        tiled=True,
    )
    return (own_rows + ffn_out).astype(jnp.bfloat16)


def solution(mesh):
    in_specs = (
        P(("grp", "hid"), None, None, None),
        P(("grp", "hid"), None, None),
        P(("grp", "hid"), "seq", None),
        P(("grp", "hid")),
        P(("grp", "hid")),
        P(("grp", "hid"), None, None),
        P(("grp", "hid"), "seq"),
        P(None, "seq"),
        P("seq"),
        P("seq", ("grp", "hid")),
        P("seq", ("grp", "hid")),
        P(("grp", "hid"), "seq"),
    )
    out_specs = P(("grp", "hid"), "seq")
    return jax.shard_map(body, mesh=mesh, in_specs=in_specs, out_specs=out_specs, check_vma=False)
```

profile of v0, /device:TPU:1, one launch (start us, length us, event | category | flops | bytes accessed | tf_op | source)
XLA Modules:
  0.0 729.6 jit_solution(17521622655844721328)
XLA Ops:
  10.0 1.3 select_reduce_fusion
  11.3 1.3 convolution_bitcast_fusion
  13.7 17.9 %all-gather.4 = f32[8,4,64]{2,1,0:T(4,128)S(1)} all-gather(f32[1,4,64]{2,1,0:T(4,128)S(1)} %bitcast.132), channel_id=3, replica_groups=mesh['grp'=2,'seq'=8,'hid'=32] {'seq'}, dimensions={0}, use_global_device_ids=true | all-gather | bytes 9216 | tf_op jit(solution)/shard_map/all_gather | solution.py:16
  31.7 11.3 %all-gather.3 = f32[8,4,64]{2,1,0:T(4,128)S(1)} all-gather(f32[1,4,64]{2,1,0:T(4,128)S(1)} %bitcast.131), channel_id=2, replica_groups=mesh['grp'=2,'seq'=8,'hid'=32] {'seq'}, dimensions={0}, use_global_device_ids=true | all-gather | bytes 9216 | tf_op jit(solution)/shard_map/all_gather | solution.py:16
  43.5 15.7 %all-gather.7.cloned.1.call-done = f32[8,4,64,512]{3,2,1,0:T(8,128)} async-done(((f32[1,4,64,512]{3,2,1,0:T(8,128)}), f32[8,4,64,512]{3,2,1,0:T(8,128)}) %all-gather.7.cloned.1.call-update) | async-done | bytes 4194320 | tf_op jit(solution)/shard_map/all_gather | solution.py:16
  59.2 1.1 slice.49
  60.3 9.1 %while.19 = (s32[]{:T(128)}, f32[1,4,64]{2,1,0:T(4,128)S(1)}, f32[1,4,64]{2,1,0:T(4,128)S(1)}, f32[1,4,64,512]{3,2,1,0:T(8,128)S(1)}, f32[8,1,4,64]{3,2,1,0:T(4,...) while((s32[]{:T(128)}, f32[1,4,64]{2,1,0:T(4,128)S(1)}, ...), condition=%wide.region_3.4_spmd, body=%wide.region_2.3_spmd.sunk | while | flops 395013 | bytes 1588371 | solution.py:21
  60.4 1.3 fusion.67
  61.7 1.2 fusion.67
  63.0 1.2 fusion.67
  64.3 1.2 fusion.67
  65.6 1.2 fusion.67
  66.9 1.2 fusion.67
  68.2 1.2 fusion.67
  70.1 34.5 %all_to_all.15 = bf16[1,4,64,512]{3,1,0,2:T(4,128)(2,1)S(1)} all-to-all(bf16[1,4,64,512]{3,1,0,2:T(4,128)(2,1)S(1)} %copy.19), channel_id=1, replica_groups=mesh['grp'=2,'seq'=8,'hid'=32] {'grp','hid'}, dimensions={2} | all-to-all | bytes 524288 | tf_op jit(solution)/shard_map/all_to_all | solution.py:123
  104.9 1.3 fusion.56
  106.3 256.0 %all-reduce.6.cloned.1.call-done = f32[256,1024]{1,0:T(8,128)} async-done(((f32[256,1024]{1,0:T(8,128)}), f32[256,1024]{1,0:T(8,128)}) %all-reduce.6.cloned.1.call-update) | async-done | bytes 1048592 | tf_op jit(solution)/shard_map/psum | solution.py:133
  362.3 1.4 multiply_reduce_fusion
  363.7 22.6 %psum.30 = bf16[256]{0:T(256)(128)(2,1)S(1)} all-reduce(bf16[256]{0:T(256)(128)(2,1)S(1)} %get-tuple-element.225), channel_id=1, replica_groups=mesh['grp'=2,'seq'=8,'hid'=32] {'seq'}, use_global_device_ids=true, to_apply=%region_9.10 | all-reduce | flops 256 | bytes 1024 | tf_op jit(solution)/shard_map/psum | solution.py:145
  388.4 66.3 %all-reduce.10.cloned.1.call-done = (bf16[256,256]{1,0:T(8,128)(2,1)}, bf16[256,256]{1,0:T(8,128)(2,1)}) async-done(((bf16[256,256]{1,0:T(8,128)(2,1)}, bf16[256,256]{1,0:T(8,128)(2,1)}), (bf16[256,256]{1,0:T(8,128)(2,1)}, bf16[256,256]{1,0:T(8,128)(2,1)})) %all-reduce.10.cloned.1.call-update) | async-done | bytes 262160 | tf_op jit(solution)/shard_map/psum | solution.py:144
  454.7 2.3 fusion.16
  457.0 1.3 dynamic-slice
  458.9 262.8 %all-reduce.8.cloned.1.call-done = f32[256,1024]{1,0:T(8,128)} async-done(((f32[256,1024]{1,0:T(8,128)}), f32[256,1024]{1,0:T(8,128)}) %all-reduce.8.cloned.1.call-update) | async-done | bytes 1048592
  721.7 1.4 fusion.24
  (71 shorter events, 7.0 us)
Async XLA Ops:
  6.5 448.1 %copy-start = (bf16[256,1024]{1,0:T(8,128)(2,1)S(1)}, bf16[256,1024]{1,0:T(8,128)(2,1)}, u32[]{:S(2)}) copy-start(bf16[256,1024]{1,0:T(8,128)(2,1)} %param.25) | copy-start | bytes 1572868
  6.5 36.4 %copy-start.6 = (bf16[1,4,576]{2,1,0:T(4,128)(2,1)S(1)}, bf16[1,4,576]{2,1,0:T(4,128)(2,1)}, u32[]{:S(2)}) copy-start(bf16[1,4,576]{2,1,0:T(4,128)(2,1)} %param.15) | copy-start | bytes 13828
  6.5 36.6 %slice-start = ((bf16[1,4,576]{2,1,0:T(4,128)(2,1)}), bf16[1,4,512]{2,1,0:T(4,128)(2,1)S(1)}, s32[]{:S(2)}) async-start(bf16[1,4,576]{2,1,0:T(4,128)(2,1)} %param.15), calls=%async_computation.5 | async-start | bytes 8192 | tf_op jit(solution)/shard_map/slice | solution.py:57
  6.5 52.7 %all-gather.7.cloned.1.call-start = ((), (), s32[]{:S(2)}) async-start(), calls=%async_computation.2 | async-start | bytes 4718592 | tf_op jit(solution)/shard_map/all_gather | solution.py:16
  13.5 348.8 %all-reduce.6.cloned.1.call-start = ((), (), s32[]{:S(2)}) async-start(), calls=%async_computation.1 | async-start | bytes 2097152 | tf_op jit(solution)/shard_map/psum | solution.py:133
  60.3 44.4 %copy-start.7 = (bf16[1,512,128]{2,1,0:T(8,128)(2,1)S(1)}, bf16[1,512,128]{2,1,0:T(8,128)(2,1)}, u32[]{:S(2)}) copy-start(bf16[1,512,128]{2,1,0:T(8,128)(2,1)} %param.19) | copy-start | bytes 393220
  60.3 44.6 %copy-start.4 = (bf16[128,1024]{1,0:T(8,128)(2,1)S(1)}, bf16[128,1024]{1,0:T(8,128)(2,1)}, u32[]{:S(2)}) copy-start(bf16[128,1024]{1,0:T(8,128)(2,1)} %param.20) | copy-start | bytes 786436
  69.4 292.9 %copy-start.3 = (bf16[256,1024]{1,0:T(8,128)(2,1)S(1)}, bf16[256,1024]{1,0:T(8,128)(2,1)}, u32[]{:S(2)}) copy-start(bf16[256,1024]{1,0:T(8,128)(2,1)} %param.21) | copy-start | bytes 1572868
  69.4 316.9 %copy-start.1 = (bf16[1024,256]{1,0:T(8,128)(2,1)S(1)}, bf16[1024,256]{1,0:T(8,128)(2,1)}, u32[]{:S(2)}) copy-start(bf16[1024,256]{1,0:T(8,128)(2,1)} %param.24) | copy-start | bytes 1572868
  69.5 316.9 %copy-start.5 = (f32[1024]{0:T(1024)S(1)}, f32[1024]{0:T(1024)}, u32[]{:S(2)}) copy-start(f32[1024]{0:T(1024)} %param.22) | copy-start | bytes 12292
  69.9 317.4 %copy-start.2 = (bf16[1024,256]{1,0:T(8,128)(2,1)S(1)}, bf16[1024,256]{1,0:T(8,128)(2,1)}, u32[]{:S(2)}) copy-start(bf16[1024,256]{1,0:T(8,128)(2,1)} %param.23) | copy-start | bytes 1572868
  106.3 348.4 %all-reduce.10.cloned.1.call-start = ((), (), s32[]{:S(2)}) async-start(), calls=%async_computation.4 | async-start | bytes 524288 | tf_op jit(solution)/shard_map/psum | solution.py:144
  388.3 333.4 %all-reduce.8.cloned.1.call-start = ((), (), s32[]{:S(2)}) async-start(), calls=%async_computation.3 | async-start | bytes 2097152
Sparse Core Ops, SparseCore 0:
  13.6 45.5 all-gather.6
  106.4 255.8 all-reduce.5
  388.4 66.1 all-reduce.9
  457.9 263.7 all-reduce.7
where the time goes:
time: 740 us; the launch traced here: 730 us
  waiting for transfers between devices  601 us (81%)
  blocking collectives  86.3 us (12%)
  between operations  15.3 us (2%)
  other arithmetic  13.2 us (2%)
  matrix products  9.05 us (1%)
    unnamed x5, waiting for transfers between devices  263 us
    psum x1, waiting for transfers between devices, body(): lax.psum(jnp.dot(flattened, output_weight, preferred_element_type=jnp.flo...  256 us
    psum x1, waiting for transfers between devices, body(): lax.psum(up_part.astype(jnp.bfloat16), 'seq').astype(jnp.float32)  66.3 us
    all_to_all x1, blocking collectives, body(): lax.all_to_all(head_out, ('grp', 'hid'), split_axis=2, concat_axis=0, til...  34.5 us
    all_gather x2, blocking collectives, joined(): gathered = jax.tree.map(lambda a: lax.all_gather(a, axis), part)  29.2 us
    psum x1, blocking collectives, body(): lax.psum(squares.astype(jnp.bfloat16), 'seq').astype(jnp.float32)  22.6 us
    all_gather x1, waiting for transfers between devices, joined(): gathered = jax.tree.map(lambda a: lax.all_gather(a, axis), part)  15.7 us
  transfers between devices with their start and end apart: 4, of which 4 were waited for; matrix products, arithmetic and copies ran while one was open for 0% of the time, Pallas kernels for 0%

commit v1 on v0

v1 whole, which is shorter than its diff:
```python
import functools
import math

import jax
import jax.numpy as jnp
from jax import lax
from jax.experimental import pallas as pl
from jax.experimental.pallas import tpu as pltpu
from jax.sharding import PartitionSpec as P

D = 8192
LATENT = 512
ROPE = 64
NX, NZ, NS = 4, 16, 8
MESH = pl.DeviceIdType.MESH
BF = jnp.bfloat16
F32 = jnp.float32
score_scale = 192.0 ** (-0.5)


def rope_tables(positions, count, halfwidth):
    counter = jnp.arange(halfwidth, dtype=F32)
    frequency = jnp.exp(counter * (-math.log(1000000.0) / halfwidth))
    places = positions.astype(F32)[:, None] + jnp.arange(count, dtype=F32)[None, :]
    angles = places[:, :, None] * frequency
    return (jnp.cos(angles), jnp.sin(angles))


def rotate(vector, cosines, sines):
    halfwidth = cosines.shape[-1]
    leading = vector[..., :halfwidth]
    trailing = vector[..., halfwidth:]
    return jnp.concatenate(
        [leading * cosines - trailing * sines, trailing * cosines + leading * sines], axis=-1
    )


def dot(a, b):
    return lax.dot_general(a, b, (((1,), (0,)), ((), ())), preferred_element_type=F32)


def dot_t(a, b):
    return lax.dot_general(a, b, (((1,), (1,)), ((), ())), preferred_element_type=F32)


def iota(shape, axis):
    return lax.broadcasted_iota(jnp.int32, shape, axis)


def one_hot(rows, cols, source_of):
    return jnp.where(iota((rows, cols), 1) == source_of(iota((rows, cols), 0)), 1.0, 0.0).astype(BF)


def remote(src, dst, send_sem, recv_sem, device):
    return pltpu.make_async_remote_copy(
        src_ref=src, dst_ref=dst, send_sem=send_sem, recv_sem=recv_sem,
        device_id=device, device_id_type=MESH,
    )


def wait_bytes(ref, sem):
    pltpu.make_async_copy(ref, ref, sem).wait()


def kernel(
    len_ref, tab_ref, newk_ref, gain_ref,
    q_hbm, k_hbm, vup_hbm, wo_hbm, res_hbm, wg_hbm, wu_hbm, wd_hbm,
    out_ref,
    q, k, vup, wo, res, wg, wu, wd,
    asend, arecv, xs, xr, zs, zr, vbuf,
    os_, orx, oz, orz, st, agb, gs, gr, hb, ds_, drx, dz, drz,
    lsem, ssem, rsem, vssem, vrsem,
):
    grp, seq, hid = lax.axis_index("grp"), lax.axis_index("seq"), lax.axis_index("hid")
    x, z = hid // 8, grp * 8 + hid % 8
    y, core = seq // 2, seq % 2

    def at(xx, zz, ss):
        return (zz // 8, ss, xx * 8 + zz % 8)

    def each(count, me, fn):
        def step(i, carry):
            fn((me + i) % count)
            return carry
        lax.fori_loop(1, count, step, 0)

    def x_peers(fn):
        each(NX, x, lambda p: fn(p, at(p, z, seq)))

    def z_peers(fn):
        each(NZ, z, lambda p: fn(p, at(x, p, seq)))

    def s_peers(fn):
        each(NS, seq, lambda p: fn(p, at(x, z, p)))

    loads = [
        pltpu.make_async_copy(a, b, lsem.at[i])
        for i, (a, b) in enumerate([
            (q_hbm, q), (k_hbm, k), (vup_hbm, vup), (wo_hbm, wo), (res_hbm, res),
            (wg_hbm, wg), (wu_hbm, wu), (wd_hbm, wd),
        ])
    ]
    for load in loads:
        load.start()

    barrier = pltpu.get_barrier_semaphore()

    def greet(p, device):
        pl.semaphore_signal(barrier, inc=1, device_id=device, device_id_type=MESH)

    x_peers(greet)
    z_peers(greet)
    s_peers(greet)

    loads[0].wait()
    loads[1].wait()
    rope_in = q[:, LATENT:]
    turn_r, turn_c = iota((ROPE, ROPE), 0), iota((ROPE, ROPE), 1)
    turn = jnp.where(
        turn_c == turn_r + 32, 1.0, jnp.where(turn_c == turn_r - 32, -1.0, 0.0)
    ).astype(BF)
    turned = dot(rope_in, turn)
    cosines = jnp.concatenate([jnp.broadcast_to(tab_ref[t:t + 1, :], (64, ROPE)) for t in range(4)], axis=0)
    sines = jnp.concatenate([jnp.broadcast_to(tab_ref[t + 4:t + 5, :], (64, ROPE)) for t in range(4)], axis=0)
    q_rope = (rope_in.astype(F32) * cosines + turned * sines).astype(BF)
    q_lat = q[:, :LATENT]
    far = (dot_t(q_lat, k[:, :LATENT]) + dot_t(q_rope, k[:, LATENT:])) * score_scale
    near = (dot_t(q_lat, newk_ref[:, :LATENT]) + dot_t(q_rope, newk_ref[:, LATENT:])) * score_scale
    usable = iota((256, 256), 1) + seq * 256 < len_ref[0]
    causal = iota((256, 16), 1) + seq * 1024 <= iota((256, 16), 0) // 64
    peak = jnp.maximum(
        jnp.max(jnp.where(usable, far, -1e30), axis=1, keepdims=True),
        jnp.max(jnp.where(causal, near, -1e30), axis=1, keepdims=True),
    )
    peak = jnp.floor(peak * (1.0 / 32.0)) * 32.0
    far_w = jnp.where(usable, jnp.exp(far - peak), 0.0)
    near_w = jnp.where(causal, jnp.exp(near - peak), 0.0)
    total = jnp.sum(far_w, axis=1, keepdims=True) + jnp.sum(near_w, axis=1, keepdims=True)
    mixture = dot(far_w.astype(BF), k[:, :LATENT]) + dot(near_w.astype(BF), newk_ref[:, :LATENT])
    asend[:, :LATENT] = mixture.astype(BF)
    lane = iota((256, 128), 1)
    high = total.astype(BF).astype(F32)
    asend[:, LATENT:] = jnp.where(
        lane == 0, peak, jnp.where(lane == 1, high, total - high)
    ).astype(BF)

    pl.semaphore_wait(barrier, (NX - 1) + (NZ - 1) + (NS - 1))

    def rows32(i):
        return pl.ds(pl.multiple_of(i * 32, 32), 32)

    s_peers(lambda p, device: remote(
        asend.at[rows32(p)], arecv.at[seq], ssem.at[0], rsem.at[0], device).start())
    arecv[seq] = asend[rows32(seq)]
    perm_one = one_hot(128, 128, lambda o: (o % 4) * 32 + o // 4)
    perm_two = one_hot(128, 128, lambda o: (o // 4 % 4) * 32 + (o // 16) * 4 + o % 4)
    wait_bytes(arecv.at[0:NS - 1], rsem.at[0])

    aux = [arecv[i, :, LATENT:].astype(F32) for i in range(NS)]
    top = functools.reduce(jnp.maximum, [a[:, 0:1] for a in aux])
    factors = [jnp.exp(a[:, 0:1] - top) for a in aux]
    totals = sum(f * (a[:, 1:2] + a[:, 2:3]) for f, a in zip(factors, aux))
    mixed = sum(f * arecv[i, :, :LATENT].astype(F32) for i, f in enumerate(factors))
    heads = (mixed / totals).astype(BF)

    stacked = jnp.concatenate([heads[:, 128 * i:128 * i + 128] for i in range(4)], axis=0)
    xs[...] = dot(perm_one, stacked).astype(BF).reshape(NX, 32, 128)
    x_peers(lambda p, device: remote(
        xs.at[p], xr.at[x], ssem.at[1], rsem.at[1], device).start())
    xr[x] = xs[x]
    wait_bytes(xr.at[0:NX - 1], rsem.at[1])
    zs[...] = dot(perm_two, xr[...].reshape(128, 128)).astype(BF).reshape(8, 16, 128)

    def to_head(j, carry):
        p = core * 8 + j

        @pl.when(p != z)
        def _():
            remote(zs.at[j], zr.at[z], ssem.at[2], rsem.at[2], at(x, p, seq)).start()

        return carry

    lax.fori_loop(0, 8, to_head, 0)

    @pl.when(grp == core)
    def _():
        zr[z] = zs[z % 8]
        perm_three = one_hot(256, 256, lambda o: (o % 16) * 16 + (o // 16 % 4) * 4 + o // 64)
        loads[2].wait()
        wait_bytes(zr.at[0:NZ - 1], rsem.at[2])
        lat = dot(perm_three, zr[...].reshape(256, 128)).astype(BF)
        value = sum(dot(lat[64 * i:64 * i + 64], vup[128 * i:128 * i + 128, :]) for i in range(4))
        vbuf[y] = value.astype(BF)

        def share(i, carry):
            p = (seq + i) % NS
            remote(vbuf.at[y], vbuf.at[y], vssem.at[i - 1], vrsem.at[y], at(x, z, p)).start()
            return carry

        lax.fori_loop(1, NS, share, 0)

    @pl.when(grp != core)
    def _():
        loads[2].wait()

    a, b = x // 2, x % 2
    u, v = z // 4, z % 4
    quad_r, quad_c = pl.ds(pl.multiple_of(a * 64, 64), 64), pl.ds(pl.multiple_of(b * 512, 512), 512)
    tile_r = pl.ds(pl.multiple_of(a * 64 + u * 16, 16), 16)
    tile_c = pl.ds(pl.multiple_of(b * 512 + v * 128, 128), 128)
    inner_r, inner_c = pl.ds(pl.multiple_of(u * 16, 16), 16), pl.ds(pl.multiple_of(v * 128, 128), 128)

    loads[3].wait()
    for c in range(2):
        for t in (2 * c, 2 * c + 1):
            @pl.when(jnp.logical_or(grp != core, y != t))
            def _():
                wait_bytes(vbuf.at[t], vrsem.at[t])
        os_[c] = dot(vbuf[2 * c:2 * c + 2].reshape(128, 128), wo[...]).astype(BF)
        x_peers(lambda p, device: remote(
            os_.at[c, pl.ds(pl.multiple_of(p // 2 * 64, 64), 64), pl.ds(pl.multiple_of(p % 2 * 512, 512), 512)],
            orx.at[c, x], ssem.at[4 + c], rsem.at[4 + c], device).start())
        orx[c, x] = os_[c, quad_r, quad_c]

    for c in range(2):
        wait_bytes(orx.at[c, 0:NX - 1], rsem.at[4 + c])
        oz[c] = sum(orx[c, i].astype(F32) for i in range(NX)).astype(BF)
        z_peers(lambda p, device: remote(
            oz.at[c, pl.ds(pl.multiple_of(p // 4 * 16, 16), 16), pl.ds(pl.multiple_of(p % 4 * 128, 128), 128)],
            orz.at[c, z], ssem.at[6 + c], rsem.at[6 + c], device).start())
        orz[c, z] = oz[c, inner_r, inner_c]

    loads[4].wait()
    gain = gain_ref[...]
    own_gain = gain_ref[:, tile_c]
    for c in range(2):
        own = one_hot(16, 256, lambda o: ((o // 8) * 32 + u * 8 + o % 8) * 4 + 2 * c + a)
        old = dot(own, res[:, tile_c])
        wait_bytes(orz.at[c, 0:NZ - 1], rsem.at[6 + c])
        stream = old + sum(orz[c, i].astype(F32) for i in range(NZ))
        st[c] = stream
        agb[c, tile_r, tile_c] = (stream * own_gain).astype(BF)
        z_peers(lambda p, device: remote(
            agb.at[c, tile_r, tile_c], agb.at[c, tile_r, tile_c],
            ssem.at[8 + c], rsem.at[8 + c], device).start())

    for c in range(2):
        wait_bytes(orz.at[c, 0:NZ - 1], rsem.at[8 + c])
        x_peers(lambda p, device: remote(
            agb.at[c, quad_r, quad_c], agb.at[c, quad_r, quad_c],
            ssem.at[10 + c], rsem.at[10 + c], device).start())

    inverse_gain = 1.0 / gain
    lane = iota((128, 128), 1)
    loads[5].wait()
    loads[6].wait()
    for c in range(2):
        wait_bytes(orx.at[c, 0:NX - 1], rsem.at[10 + c])
        scaled = agb[c]
        gs[c, :, 0:256] = dot(scaled, wg[...]).astype(BF)
        gs[c, :, 256:512] = dot(scaled, wu[...]).astype(BF)
        plain = scaled.astype(F32) * inverse_gain
        squares = jnp.sum(plain * plain, axis=1, keepdims=True)
        high = squares.astype(BF).astype(F32)
        gs[c, :, 512:640] = jnp.where(lane == 0, high, squares - high).astype(BF)

        def rows16(i):
            return pl.ds(pl.multiple_of(i * 16, 16), 16)

        s_peers(lambda p, device: remote(
            gs.at[c, rows16(p)], gr.at[c, seq], ssem.at[12 + c], rsem.at[12 + c], device).start())
        gr[c, seq] = gs[c, rows16(seq)]

    for c in range(2):
        wait_bytes(gr.at[c, 0:NS - 1], rsem.at[12 + c])
        sums = sum(gr[c, i].astype(F32) for i in range(NS))
        square = sums[:, 512:513] + sums[:, 513:514]
        inverse = lax.rsqrt(square * (1.0 / D) + 1e-06)
        gate = sums[:, 0:256] * inverse
        up = sums[:, 256:512] * inverse
        mine = rows16(seq)
        hb[c, mine] = (gate / (1.0 + jnp.exp(-gate)) * up).astype(BF)
        s_peers(lambda p, device: remote(
            hb.at[c, mine], hb.at[c, mine], ssem.at[14 + c], rsem.at[14 + c], device).start())

    loads[7].wait()
    perm_four = one_hot(256, 256, lambda o: (o // 2 % 8) * 32 + (o % 2) * 16 + o // 16)
    for c in range(2):
        wait_bytes(hb.at[c, 0:112], rsem.at[14 + c])
        part = dot(hb[c], wd[...])
        ds_[c] = part.astype(BF).reshape(2, 64, 1024)
        mine_r, mine_c = pl.ds(pl.multiple_of(u * 16, 16), 16), tile_c
        own = dot(hb[c, tile_r, :], wd[:, tile_c]) + st[c]
        ds_[c, a, mine_r, mine_c] = own.astype(BF)
        x_peers(lambda p, device: remote(
            ds_.at[c, :, pl.ds(pl.multiple_of(p * 16, 16), 16)], drx.at[c, x],
            ssem.at[16 + c], rsem.at[16 + c], device).start())
        drx[c, x] = ds_[c, :, pl.ds(pl.multiple_of(x * 16, 16), 16)]

    for c in range(2):
        wait_bytes(drx.at[c, 0:NX - 1], rsem.at[16 + c])
        summed = sum(drx[c, i].astype(F32) for i in range(NX)).astype(BF).reshape(32, 1024)
        stacked = jnp.concatenate([summed[:, 128 * i:128 * i + 128] for i in range(8)], axis=0)
        dz[c] = dot(perm_four, stacked).astype(BF).reshape(NZ, 16, 128)
        z_peers(lambda p, device: remote(
            dz.at[c, p], drz.at[c, z], ssem.at[18 + c], rsem.at[18 + c], device).start())
        drz[c, z] = dz[c, z]

    for c in range(2):
        wait_bytes(drz.at[c, 0:NZ - 1], rsem.at[18 + c])
        out_ref[c] = sum(drz[c, i].astype(F32) for i in range(NZ)).astype(BF)

    wait_bytes(arecv.at[0:NS - 1], ssem.at[0])
    wait_bytes(xr.at[0:NX - 1], ssem.at[1])

    @pl.when(grp == core)
    def _():
        wait_bytes(zs.at[0:7], ssem.at[2])

        def shared(i, carry):
            wait_bytes(vbuf.at[y], vssem.at[i - 1])
            return carry

        lax.fori_loop(1, NS, shared, 0)

    @pl.when(grp != core)
    def _():
        wait_bytes(zs, ssem.at[2])

    for c in range(2):
        wait_bytes(orx.at[c, 0:NX - 1], ssem.at[4 + c])
        wait_bytes(orz.at[c, 0:NZ - 1], ssem.at[6 + c])
        wait_bytes(orz.at[c, 0:NZ - 1], ssem.at[8 + c])
        wait_bytes(orx.at[c, 0:NX - 1], ssem.at[10 + c])
        wait_bytes(gr.at[c, 0:NS - 1], ssem.at[12 + c])
        wait_bytes(hb.at[c, 0:112], ssem.at[14 + c])
        wait_bytes(drx.at[c, 0:NX - 1], ssem.at[16 + c])
        wait_bytes(drz.at[c, 0:NZ - 1], ssem.at[18 + c])


def body(
    queries, new_latents, latent_cache, lengths, positions, value_up,
    output_weight, residual, norm_gain, gate_weight, up_weight, down_weight,
):
    cosines, sines = rope_tables(positions, 4, ROPE // 2)
    key_rope = rotate(new_latents[..., LATENT:].astype(F32), cosines, sines)
    new_keys = jnp.concatenate([new_latents[..., :LATENT], key_rope.astype(BF)], axis=-1)
    new_keys = jnp.pad(new_keys[0], ((0, 12), (0, 0)))
    both = jnp.concatenate([cosines[0], sines[0]], axis=0)
    table = jnp.concatenate([both, both], axis=1)
    vmem, hbm = pl.BlockSpec(memory_space=pltpu.VMEM), pl.BlockSpec(memory_space=pl.ANY)

    def buf(*shape, dtype=BF):
        return pltpu.VMEM(shape, dtype)

    out = pl.pallas_call(
        kernel,
        out_shape=jax.ShapeDtypeStruct((2, 16, 128), BF),
        in_specs=[pl.BlockSpec(memory_space=pltpu.SMEM), vmem, vmem, vmem] + [hbm] * 8,
        out_specs=vmem,
        scratch_shapes=[
            buf(256, 576), buf(256, 576), buf(512, 128), buf(128, 1024), buf(256, 1024),
            buf(1024, 256), buf(1024, 256), buf(256, 1024),
            buf(256, 640), buf(NS, 32, 640),
            buf(NX, 32, 128), buf(NX, 32, 128), buf(8, 16, 128), buf(NZ, 16, 128), buf(4, 64, 128),
            buf(2, 128, 1024), buf(2, NX, 64, 512), buf(2, 64, 512), buf(2, NZ, 16, 128),
            buf(2, 16, 128, dtype=F32), buf(2, 128, 1024),
            buf(2, 128, 640), buf(2, NS, 16, 640), buf(2, 128, 256),
            buf(2, 2, 64, 1024), buf(2, NX, 2, 16, 1024), buf(2, NZ, 16, 128), buf(2, NZ, 16, 128),
            pltpu.SemaphoreType.DMA((8,)),
            pltpu.SemaphoreType.DMA((20,)),
            pltpu.SemaphoreType.DMA((20,)),
            pltpu.SemaphoreType.DMA((NS - 1,)),
            pltpu.SemaphoreType.DMA((4,)),
        ],
        compiler_params=pltpu.CompilerParams(
            collective_id=0, has_side_effects=True, vmem_limit_bytes=40 * 1024 * 1024,
        ),
        cost_estimate=pl.CostEstimate(flops=10**9, bytes_accessed=4 * 10**6, transcendentals=10**5),
    )(
        lengths, table, new_keys, norm_gain.reshape(1, -1),
        queries.reshape(256, 576), latent_cache.reshape(256, 576), value_up.reshape(512, 128),
        output_weight, residual, gate_weight, up_weight, down_weight,
    )
    return out.reshape(2, 8, 2, 128).transpose(0, 2, 1, 3).reshape(4, 1024)


def solution(mesh):
    rows = ("grp", "hid")
    in_specs = (
        P(rows, None, None, None),
        P(rows, None, None),
        P(rows, "seq", None),
        P(rows),
        P(rows),
        P(rows, None, None),
        P(rows, "seq"),
        P(None, "seq"),
        P("seq"),
        P("seq", rows),
        P("seq", rows),
        P(rows, "seq"),
    )
    return jax.shard_map(body, mesh=mesh, in_specs=in_specs, out_specs=P(rows, "seq"), check_vma=False)
```

time: 740 us -> 102 us (0.14); the launches traced: 730 us -> 102 us
  waiting for transfers between devices: 601 us -> 0 us
  Pallas kernels: 0 us -> 91.6 us
  blocking collectives: 86.3 us -> 0 us
  between operations: 15.3 us -> 1.44 us
  other arithmetic: 13.2 us -> 1.08 us
  matrix products: 9.05 us -> 0 us
    psum x2 -> x0, waiting for transfers between devices: 322 us -> none  [the longest x1 256 us: body(): lax.psum(jnp.dot(flattened, output_weight, preferred_element_type=jnp.flo...]
    unnamed x5 -> x0, waiting for transfers between devices: 263 us -> none
    pallas_call x0 -> x1, Pallas kernels: none -> 91.6 us  [body(): pl.pallas_call(kernel, out_shape=jax.ShapeDtypeStruct((2, 16, 128), BF),...]
    all_to_all x1 -> x0, blocking collectives: 34.5 us -> none  [body(): lax.all_to_all(head_out, ('grp', 'hid'), split_axis=2, concat_axis=0, til...]
    all_gather x2 -> x0, blocking collectives: 29.2 us -> none  [joined(): gathered = jax.tree.map(lambda a: lax.all_gather(a, axis), part)]
    psum x1 -> x0, blocking collectives: 22.6 us -> none  [body(): lax.psum(squares.astype(jnp.bfloat16), 'seq').astype(jnp.float32)]
    all_gather x1 -> x0, waiting for transfers between devices: 15.7 us -> none  [joined(): gathered = jax.tree.map(lambda a: lax.all_gather(a, axis), part)]
    dot_general x9 -> x0, matrix products: 9.05 us -> none  [the longest x1 2.31 us: body(): jnp.dot(hidden, down_weight, preferred_element_type=jnp.float32)]
  transfers between devices with their start and end apart: 4 -> 0, of which waited for: 4 -> 0; matrix products, arithmetic and copies ran while one was open for 0% -> 0% of each run, Pallas kernels for 0% -> 0%
where the time goes in v1:
time: 102 us
  Pallas kernels  91.6 us (90%)
  local copies, waits for them, and re-layouts  7.57 us (7%)
  between operations  1.44 us (1%)
  other arithmetic  1.08 us (1%)
    pallas_call x1, Pallas kernels, body(): pl.pallas_call(kernel, out_shape=jax.ShapeDtypeStruct((2, 16, 128), BF),...  91.6 us
    unnamed x18, local copies, waits for them, and re-layouts  6.85 us

profile of v1, /device:TPU:1, one launch (start us, length us, event | category | flops | bytes accessed | tf_op | source)
XLA Modules:
  0.0 101.6 jit_solution(3277932247869892141)
XLA Ops:
  0.0 0.0 copy-start
  1.4 0.7 slice_convert_fusion
  2.1 0.1 fusion.5
  2.2 0.1 multiply_cosine_fusion.1
  2.3 0.1 maximum_maximum_fusion.tab_ref
  2.4 0.7 slice.12
  3.1 0.1 maximum_bitcast_fusion
  3.2 0.0 copy-start.6
  3.2 0.0 copy-start.7
  3.2 1.2 %copy.13 = bf16[1,256,576]{2,1,0:T(8,128)(2,1)S(1)} copy(bf16[1,256,576]{1,2,0:T(8,128)(2,1)} %param.14) | data formatting | bytes 589824 | tf_op args[2]
  4.4 0.0 copy-done
  4.4 0.0 copy-done.6
  4.4 0.0 copy-done.7
  4.4 0.0 copy-start.1
  4.4 1.0 %copy-done.1 = bf16[1024,256]{1,0:T(8,128)(2,1)S(1)} copy-done((bf16[1024,256]{1,0:T(8,128)(2,1)S(1)}, bf16[1024,256]{1,0:T(8,128)(2,1)}, u32[]{:S(2)}) %copy-start.1) | copy-done | bytes 524312
  5.5 0.0 copy-start.2
  5.5 1.0 %copy-done.2 = bf16[1024,256]{1,0:T(8,128)(2,1)S(1)} copy-done((bf16[1024,256]{1,0:T(8,128)(2,1)S(1)}, bf16[1024,256]{1,0:T(8,128)(2,1)}, u32[]{:S(2)}) %copy-start.2) | copy-done | bytes 524312
  6.5 0.0 copy-start.3
  6.5 1.0 %copy-done.3 = bf16[256,1024]{1,0:T(8,128)(2,1)S(1)} copy-done((bf16[256,1024]{1,0:T(8,128)(2,1)S(1)}, bf16[256,1024]{1,0:T(8,128)(2,1)}, u32[]{:S(2)}) %copy-start.3) | copy-done | bytes 524312
  7.5 1.0 copy-done.4
  8.5 0.0 copy-start.5
  8.5 0.9 copy-done.5
  9.5 91.6 %shard_map.118 = bf16[2,16,128]{2,1,0:T(8,128)(2,1)S(1)} custom-call(s32[1]{0:T(128)S(6)} %copy.18.len_ref, f32[8,64]{1,0:T(8,128)S(1)} %maximum_maximum_fusion.tab_ref, bf16[16,576]{1,0:T(8,128)(2,1)S(1)} %pad.4.newk_ref, f32[1,1024]{1,0:T(1,128)S(1)} %bitcast.19, bf16[256,576]{1,0:T(8,128)(2,1)S(1)} %bitcast.17, bf16[256,576]{1,0:T(8,128)(2,1)S(1)} %bitcast.15, ...), custom_call_target="tpu_custom_call" | custom-call | flops 1000000000 | bytes 4000000 | tf_op jit(solution)/shard_map/pallas_call | solution.py:356
  101.0 0.6 copy.17
  (5 shorter events, 0.0 us)
Async XLA Ops:
  0.0 4.4 %copy-start = (bf16[256,1024]{1,0:T(8,128)(2,1)S(1)}, bf16[256,1024]{1,0:T(8,128)(2,1)}, u32[]{:S(2)}) copy-start(bf16[256,1024]{1,0:T(8,128)(2,1)} %res_hbm.1) | copy-start | bytes 1572868
  3.2 1.2 %copy-start.6 = (bf16[1,512,128]{2,1,0:T(8,128)(2,1)S(1)}, bf16[1,512,128]{2,1,0:T(8,128)(2,1)}, u32[]{:S(2)}) copy-start(bf16[1,512,128]{2,1,0:T(8,128)(2,1)} %param.17) | copy-start | bytes 393220
  3.2 1.2 %copy-start.7 = (f32[1024]{0:T(1024)S(1)}, f32[1024]{0:T(1024)}, u32[]{:S(2)}) copy-start(f32[1024]{0:T(1024)} %param.20) | copy-start | bytes 12292
  4.4 1.0 %copy-start.1 = (bf16[1024,256]{1,0:T(8,128)(2,1)S(1)}, bf16[1024,256]{1,0:T(8,128)(2,1)}, u32[]{:S(2)}) copy-start(bf16[1024,256]{1,0:T(8,128)(2,1)} %wg_hbm.1) | copy-start | bytes 1572868
  5.5 1.0 %copy-start.2 = (bf16[1024,256]{1,0:T(8,128)(2,1)S(1)}, bf16[1024,256]{1,0:T(8,128)(2,1)}, u32[]{:S(2)}) copy-start(bf16[1024,256]{1,0:T(8,128)(2,1)} %wu_hbm.1) | copy-start | bytes 1572868
  6.5 1.0 %copy-start.3 = (bf16[256,1024]{1,0:T(8,128)(2,1)S(1)}, bf16[256,1024]{1,0:T(8,128)(2,1)}, u32[]{:S(2)}) copy-start(bf16[256,1024]{1,0:T(8,128)(2,1)} %wd_hbm.1) | copy-start | bytes 1572868
  7.5 1.0 copy-start.4
  8.5 0.9 copy-start.5

commit v2 on v1

v2 whole, which is shorter than its diff:
```python
import functools

import jax
import jax.numpy as jnp
import numpy as np
from jax import lax
from jax.experimental import pallas as pl
from jax.experimental.pallas import tpu as pltpu
from jax.sharding import PartitionSpec as P

D = 8192
LATENT = 512
ROPE = 64
NX, NZ, NS = 4, 16, 8
MESH = pl.DeviceIdType.MESH
BF = jnp.bfloat16
F32 = jnp.float32
score_scale = 192.0 ** (-0.5)


def dot(a, b):
    return lax.dot_general(a, b, (((1,), (0,)), ((), ())), preferred_element_type=F32)


def dot_t(a, b):
    return lax.dot_general(a, b, (((1,), (1,)), ((), ())), preferred_element_type=F32)


def iota(shape, axis):
    return lax.broadcasted_iota(jnp.int32, shape, axis)


def one_hot(rows, cols, source_of):
    return jnp.where(iota((rows, cols), 1) == source_of(iota((rows, cols), 0)), 1.0, 0.0).astype(BF)


def remote(src, dst, send_sem, recv_sem, device):
    return pltpu.make_async_remote_copy(
        src_ref=src, dst_ref=dst, send_sem=send_sem, recv_sem=recv_sem,
        device_id=device, device_id_type=MESH,
    )


def wait_bytes(ref, sem):
    pltpu.make_async_copy(ref, ref, sem).wait()


def kernel(
    freq_hbm, pos_hbm, len_hbm, new_hbm, gain_hbm,
    q_hbm, k_hbm, vup_hbm, wo_hbm, res_hbm, wg_hbm, wu_hbm, wd_hbm,
    out_ref,
    freq_ref, pos_ref, len_ref, new_ref, gain_ref,
    q, kt, vup, wo, res, wg, wu, wd,
    asend, arecv, zs, zr, vbuf, ob, orz, st, agb, gs, gr, hb,
    ds_, drx, dz, drz,
    lsem, ssem, rsem, fsem,
):
    grp, seq, hid = lax.axis_index("grp"), lax.axis_index("seq"), lax.axis_index("hid")
    x, z = hid // 8, grp * 8 + hid % 8
    y, core = seq // 2, seq % 2

    def at(xx, zz, ss):
        return (zz // 8, ss, xx * 8 + zz % 8)

    def each(count, me, fn):
        def step(i, carry):
            fn((me + i) % count)
            return carry
        lax.fori_loop(1, count, step, 0)

    def x_peers(fn):
        each(NX, x, lambda p: fn(p, at(p, z, seq)))

    def s_peers(fn):
        each(NS, seq, lambda p: fn(p, at(x, z, p)))

    def z_distance(i):
        return 8 + (1 - 2 * (i % 2)) * (i // 2)

    def z_peers(fn):
        def step(i, carry):
            p = (z + z_distance(i)) % NZ
            fn(p, at(x, p, seq))
            return carry
        lax.fori_loop(1, NZ, step, 0)

    def xs_peers(fn):
        for dx in (2, 1, 3, 0):
            def step(i, carry):
                p, r = (x + dx) % NX, (seq + i) % NS
                fn(p, at(p, z, r))
                return carry
            lax.fori_loop(1 if dx == 0 else 0, NS, step, 0)

    def rows(i, n):
        return pl.ds(pl.multiple_of(i * n, n), n)

    own_cols = rows(x, 256)
    loads = [
        pltpu.make_async_copy(a, b, lsem.at[i])
        for i, (a, b) in enumerate([
            (q_hbm, q), (k_hbm, kt), (vup_hbm, vup.at[x]), (wo_hbm.at[:, own_cols], wo.at[x]), (res_hbm, res),
            (wg_hbm, wg), (wu_hbm, wu), (wd_hbm, wd),
            (freq_hbm, freq_ref), (pos_hbm, pos_ref), (len_hbm, len_ref),
            (new_hbm, new_ref), (gain_hbm, gain_ref),
        ])
    ]
    for load in loads:
        load.start()

    barrier = pltpu.get_barrier_semaphore()

    def greet(p, device):
        pl.semaphore_signal(barrier, inc=1, device_id=device, device_id_type=MESH)

    xs_peers(greet)
    z_peers(greet)

    loads[8].wait()
    loads[9].wait()
    places = (pos_ref[0] + iota((8, 128), 0)).astype(F32)
    angles = places * freq_ref[...]
    cos_table, sin_table = jnp.cos(angles), jnp.sin(angles)
    loads[0].wait()
    rope_in = q[:, LATENT:]
    turn_r, turn_c = iota((ROPE, ROPE), 0), iota((ROPE, ROPE), 1)
    turn = jnp.where(
        turn_c == turn_r + 32, 1.0, jnp.where(turn_c == turn_r - 32, -1.0, 0.0)
    ).astype(BF)
    turned = dot(rope_in, turn)
    cosines = jnp.concatenate([jnp.broadcast_to(cos_table[t:t + 1, :ROPE], (64, ROPE)) for t in range(4)], axis=0)
    sines = jnp.concatenate([jnp.broadcast_to(sin_table[t:t + 1, :ROPE], (64, ROPE)) for t in range(4)], axis=0)
    q_rope = (rope_in.astype(F32) * cosines + turned * sines).astype(BF)
    q_lat = q[:, :LATENT]
    loads[11].wait()
    fresh = new_ref[...].astype(F32)
    fresh = jnp.concatenate([fresh, jnp.zeros((4, LATENT + ROPE), F32)], axis=0)
    fresh_in = fresh[:, LATENT:]
    fresh_turned = dot(fresh_in.astype(BF), turn)
    fresh_rope = fresh_in * cos_table[:, :ROPE] + fresh_turned * sin_table[:, :ROPE]
    new_lat = jnp.concatenate([fresh[:, :LATENT], jnp.zeros((8, LATENT), F32)], axis=0).astype(BF)
    new_rope = jnp.concatenate([fresh_rope, jnp.zeros((8, ROPE), F32)], axis=0).astype(BF)
    near = (dot_t(q_lat, new_lat) + dot_t(q_rope, new_rope)) * score_scale
    loads[1].wait()
    loads[10].wait()
    far = (dot(q_lat, kt[:LATENT, :]) + dot(q_rope, kt[LATENT:, :])) * score_scale
    usable = iota((256, 256), 1) + seq * 256 < len_ref[0]
    causal = iota((256, 16), 1) + seq * 1024 <= iota((256, 16), 0) // 64
    peak = jnp.maximum(
        jnp.max(jnp.where(usable, far, -1e30), axis=1, keepdims=True),
        jnp.max(jnp.where(causal, near, -1e30), axis=1, keepdims=True),
    )
    peak = jnp.floor(peak * (1.0 / 32.0)) * 32.0
    far_w = jnp.where(usable, jnp.exp(far - peak), 0.0)
    near_w = jnp.where(causal, jnp.exp(near - peak), 0.0)
    total = jnp.sum(far_w, axis=1, keepdims=True) + jnp.sum(near_w, axis=1, keepdims=True)
    mixture = dot_t(far_w.astype(BF), kt[:LATENT, :]) + dot(near_w.astype(BF), new_lat)
    asend[:, :LATENT] = mixture.astype(BF)
    lane = iota((256, 128), 1)
    high = total.astype(BF).astype(F32)
    asend[:, LATENT:] = jnp.where(
        lane == 0, peak, jnp.where(lane == 1, high, total - high)
    ).astype(BF)

    pl.semaphore_wait(barrier, (NX * NS - 1) + (NZ - 1))
    s_peers(lambda p, device: remote(
        asend.at[rows(p, 32)], arecv.at[seq], ssem.at[0], rsem.at[0], device).start())

    x_peers(lambda p, device: remote(
        vup_hbm, vup.at[x], ssem.at[1], rsem.at[1], device).start())
    x_peers(lambda p, device: remote(
        wo_hbm.at[:, rows(p, 256)], wo.at[x], ssem.at[2], rsem.at[2], device).start())

    arecv[seq] = asend[rows(seq, 32)]
    perm_one = one_hot(128, 128, lambda o: (o % 4) * 32 + (o // 4 % 4) * 8 + o // 16)
    perm_two = one_hot(256, 256, lambda o: (o % 16) * 16 + o // 16)
    wait_bytes(arecv.at[0:NS - 1], rsem.at[0])

    aux = [arecv[i, :, LATENT:].astype(F32) for i in range(NS)]
    top = functools.reduce(jnp.maximum, [a[:, 0:1] for a in aux])
    factors = [jnp.exp(a[:, 0:1] - top) for a in aux]
    totals = sum(f * (a[:, 1:2] + a[:, 2:3]) for f, a in zip(factors, aux))
    mixed = sum(f * arecv[i, :, :LATENT].astype(F32) for i, f in enumerate(factors))
    heads = (mixed / totals).astype(BF)

    stacked = jnp.concatenate([heads[:, 128 * i:128 * i + 128] for i in range(4)], axis=0)
    zs[...] = dot(perm_one, stacked).astype(BF).reshape(8, 16, 128)

    def to_head(j, carry):
        p = core * 8 + j

        @pl.when(p != z)
        def _():
            remote(zs.at[j], zr.at[z], ssem.at[3], rsem.at[3], at(x, p, seq)).start()

        return carry

    lax.fori_loop(0, 8, to_head, 0)
    loads[2].wait()
    wait_bytes(vup.at[0:NX - 1], rsem.at[1])
    value_rows = rows(y * 4 + x, 16)

    @pl.when(grp == core)
    def _():
        zr[z] = zs[z % 8]
        wait_bytes(zr.at[0:NZ - 1], rsem.at[3])
        lat = dot(perm_two, zr[...].reshape(256, 128)).astype(BF)
        for i in range(NX):
            wide = jnp.concatenate([lat[64 * i + 16 * n:64 * i + 16 * n + 16] for n in range(4)], axis=1)
            vbuf[value_rows, 128 * i:128 * i + 128] = dot(wide, vup[i]).astype(BF)
        xs_peers(lambda p, device: remote(
            vbuf.at[value_rows], vbuf.at[value_rows], ssem.at[4], rsem.at[4], device).start())

    loads[3].wait()
    wait_bytes(wo.at[0:NX - 1], rsem.at[2])

    @pl.when(grp == core)
    def _():
        wait_bytes(vbuf.at[0:240], rsem.at[4])

    @pl.when(grp != core)
    def _():
        wait_bytes(vbuf, rsem.at[4])

    ob[...] = dot(vbuf[...], wo[...].reshape(512, 256)).astype(BF)
    z_peers(lambda p, device: remote(
        ob.at[rows(p, 16)], orz.at[z], ssem.at[5], rsem.at[5], device).start())
    tile = rows(z, 16)
    orz[z] = ob[tile]
    loads[4].wait()
    loads[12].wait()
    gain = gain_ref[...]
    own = one_hot(16, 256, lambda o: ((o // 8) * 32 + (z % 4) * 8 + o % 8) * 4 + z // 4)
    old = dot(own, res[:, own_cols])
    wait_bytes(orz.at[0:NZ - 1], rsem.at[5])
    stream = old + sum(orz[i].astype(F32) for i in range(NZ))
    st[...] = stream
    agb[tile, own_cols] = (stream * gain_ref[:, own_cols]).astype(BF)
    z_peers(lambda p, device: remote(
        agb.at[tile, own_cols], agb.at[tile, own_cols], ssem.at[6], fsem.at[z], device).start())

    def forward(p):
        piece = agb.at[rows(p, 16), own_cols]
        x_peers(lambda _, device: remote(piece, piece, ssem.at[7], rsem.at[7], device).start())

    def arrived(i, carry):
        p = (z + z_distance(NZ - i)) % NZ
        wait_bytes(agb.at[rows(p, 16), own_cols], fsem.at[p])
        forward(p)
        return carry

    forward(z)
    lax.fori_loop(1, NZ, arrived, 0)

    inverse_gain = 1.0 / gain
    lane = iota((256, 128), 1)
    loads[5].wait()
    loads[6].wait()
    wait_bytes(agb.at[0:192], rsem.at[7])
    scaled = agb[...]
    gs[:, 0:256] = dot(scaled, wg[...]).astype(BF)
    gs[:, 256:512] = dot(scaled, wu[...]).astype(BF)
    plain = scaled.astype(F32) * inverse_gain
    squares = jnp.sum(plain * plain, axis=1, keepdims=True)
    high = squares.astype(BF).astype(F32)
    gs[:, 512:640] = jnp.where(lane == 0, high, squares - high).astype(BF)
    s_peers(lambda p, device: remote(
        gs.at[rows(p, 32)], gr.at[seq], ssem.at[8], rsem.at[8], device).start())
    mine = rows(seq, 32)
    gr[seq] = gs[mine]

    wait_bytes(gr.at[0:NS - 1], rsem.at[8])
    sums = sum(gr[i].astype(F32) for i in range(NS))
    square = sums[:, 512:513] + sums[:, 513:514]
    inverse = lax.rsqrt(square * (1.0 / D) + 1e-06)
    gate = sums[:, 0:256] * inverse
    up = sums[:, 256:512] * inverse
    hb[mine] = (gate / (1.0 + jnp.exp(-gate)) * up).astype(BF)
    s_peers(lambda p, device: remote(
        hb.at[mine], hb.at[mine], ssem.at[9], rsem.at[9], device).start())

    loads[7].wait()
    perm_four = one_hot(256, 256, lambda o: (o // 2 % 8) * 32 + (o % 2) * 16 + o // 16)
    wait_bytes(hb.at[0:224], rsem.at[9])
    for c in range(2):
        ds_[c] = dot(hb[128 * c:128 * c + 128], wd[...]).astype(BF).reshape(2, 64, 1024)

        @pl.when(grp == c)
        def _():
            own = dot(hb[tile], wd[:, own_cols]) + st[...]
            ds_[c, z // 4 % 2, rows(z % 4, 16), own_cols] = own.astype(BF)

        x_peers(lambda p, device: remote(
            ds_.at[c, :, pl.ds(pl.multiple_of(p * 16, 16), 16)], drx.at[c, x],
            ssem.at[10 + c], rsem.at[10 + c], device).start())
        drx[c, x] = ds_[c, :, pl.ds(pl.multiple_of(x * 16, 16), 16)]

    for c in range(2):
        wait_bytes(drx.at[c, 0:NX - 1], rsem.at[10 + c])
        summed = sum(drx[c, i].astype(F32) for i in range(NX)).astype(BF).reshape(32, 1024)
        stacked = jnp.concatenate([summed[:, 128 * i:128 * i + 128] for i in range(8)], axis=0)
        dz[c] = dot(perm_four, stacked).astype(BF).reshape(NZ, 16, 128)
        z_peers(lambda p, device: remote(
            dz.at[c, p], drz.at[c, z], ssem.at[12 + c], rsem.at[12 + c], device).start())
        drz[c, z] = dz[c, z]

    for c in range(2):
        wait_bytes(drz.at[c, 0:NZ - 1], rsem.at[12 + c])
        final = sum(drz[c, i].astype(F32) for i in range(NZ)).astype(BF)
        for i in range(8):
            out_ref[2 * c:2 * c + 2, 128 * i:128 * i + 128] = final[2 * i:2 * i + 2]

    wait_bytes(arecv.at[0:NS - 1], ssem.at[0])
    wait_bytes(vup.at[0:NX - 1], ssem.at[1])
    wait_bytes(wo.at[0:NX - 1], ssem.at[2])

    @pl.when(grp == core)
    def _():
        wait_bytes(zs.at[0:7], ssem.at[3])
        wait_bytes(wg.at[0:992], ssem.at[4])

    @pl.when(grp != core)
    def _():
        wait_bytes(zs, ssem.at[3])

    wait_bytes(orz.at[0:NZ - 1], ssem.at[5])
    wait_bytes(orz.at[0:NZ - 1], ssem.at[6])
    wait_bytes(agb.at[0:192], ssem.at[7])
    wait_bytes(gr.at[0:NS - 1], ssem.at[8])
    wait_bytes(hb.at[0:224], ssem.at[9])
    for c in range(2):
        wait_bytes(drx.at[c, 0:NX - 1], ssem.at[10 + c])
        wait_bytes(drz.at[c, 0:NZ - 1], ssem.at[12 + c])


def body(
    queries, new_latents, latent_cache, lengths, positions, value_up,
    output_weight, residual, norm_gain, gate_weight, up_weight, down_weight,
):
    halfwidth = ROPE // 2
    frequency = 1000000.0 ** (-np.arange(halfwidth, dtype=np.float64) / halfwidth)
    frequency = jnp.asarray(np.tile(frequency, 4)[None, :], F32)
    vmem, hbm = pl.BlockSpec(memory_space=pltpu.VMEM), pl.BlockSpec(memory_space=pltpu.HBM)

    def buf(*shape, dtype=BF):
        return pltpu.VMEM(shape, dtype)

    return pl.pallas_call(
        kernel,
        out_shape=jax.ShapeDtypeStruct((4, 1024), BF),
        in_specs=[hbm] * 13,
        out_specs=vmem,
        scratch_shapes=[
            buf(1, 128, dtype=F32), pltpu.SMEM((1,), jnp.int32), pltpu.SMEM((1,), jnp.int32),
            buf(4, 576), buf(1, 1024, dtype=F32),
            buf(256, 576), buf(576, 256), buf(NX, 512, 128), buf(NX, 128, 256), buf(256, 1024),
            buf(1024, 256), buf(1024, 256), buf(256, 1024),
            buf(256, 640), buf(NS, 32, 640), buf(8, 16, 128), buf(NZ, 16, 128),
            buf(256, 512), buf(256, 256), buf(NZ, 16, 256), buf(16, 256, dtype=F32), buf(256, 1024),
            buf(256, 640), buf(NS, 32, 640), buf(256, 256),
            buf(2, 2, 64, 1024), buf(2, NX, 2, 16, 1024), buf(2, NZ, 16, 128), buf(2, NZ, 16, 128),
            pltpu.SemaphoreType.DMA((13,)),
            pltpu.SemaphoreType.DMA((14,)),
            pltpu.SemaphoreType.DMA((14,)),
            pltpu.SemaphoreType.DMA((NZ,)),
        ],
        compiler_params=pltpu.CompilerParams(
            collective_id=0, has_side_effects=True, vmem_limit_bytes=56 * 1024 * 1024,
        ),
        cost_estimate=pl.CostEstimate(flops=10**9, bytes_accessed=4 * 10**6, transcendentals=10**5),
    )(
        frequency, positions, lengths, new_latents.reshape(4, 576), norm_gain.reshape(1, -1),
        queries.reshape(256, 576), jnp.swapaxes(latent_cache.reshape(256, 576), 0, 1), value_up.reshape(512, 128),
        output_weight, residual, gate_weight, up_weight, down_weight,
    )


def solution(mesh):
    rows = ("grp", "hid")
    in_specs = (
        P(rows, None, None, None),
        P(rows, None, None),
        P(rows, "seq", None),
        P(rows),
        P(rows),
        P(rows, None, None),
        P(rows, "seq"),
        P(None, "seq"),
        P("seq"),
        P("seq", rows),
        P("seq", rows),
        P(rows, "seq"),
    )
    return jax.shard_map(body, mesh=mesh, in_specs=in_specs, out_specs=P(rows, "seq"), check_vma=False)
```

time: 102 us -> 91.1 us (0.89)
  local copies, waits for them, and re-layouts: 7.57 us -> 1.3 us
  Pallas kernels: 91.6 us -> 88.3 us
  other arithmetic: 1.08 us -> 0 us
    unnamed x18 -> x1, local copies, waits for them, and re-layouts: 6.85 us -> 1.3 us
    pallas_call x1, Pallas kernels: 91.6 us -> 88.3 us  [body(): pl.pallas_call(kernel, out_shape=jax.ShapeDtypeStruct((4, 1024), BF), in_...]
where the time goes in v2:
time: 91.1 us; the launch traced here: 90.9 us
  Pallas kernels  88.3 us (97%)
  local copies, waits for them, and re-layouts  1.3 us (1%)
  between operations  1.3 us (1%)
    pallas_call x1, Pallas kernels, body(): pl.pallas_call(kernel, out_shape=jax.ShapeDtypeStruct((4, 1024), BF), in_...  88.3 us

profile of v2, /device:TPU:1, one launch (start us, length us, event | category | flops | bytes accessed | tf_op | source)
XLA Modules:
  0.0 90.9 jit_solution(5460304977373954941)
XLA Ops:
  1.3 88.3 %shard_map.127 = bf16[4,1024]{1,0:T(4,128)(2,1)} custom-call(f32[1,128]{1,0:T(1,128)} %constant.2.clone.freq_hbm, s32[1]{0:T(128)S(6)} %copy.16.pos_hbm, s32[1]{0:T(128)S(6)} %copy.15.len_hbm, bf16[4,576]{1,0:T(4,128)(2,1)} %bitcast.10, f32[1,1024]{1,0:T(1,128)} %bitcast.11, bf16[256,576]{1,0:T(8,128)(2,1)} %bitcast.7, bf16[576,256]{1,0:T(8,128)(2,1)} %bitcast.8, ...), custom_call_target="tpu_custom_call" | custom-call | flops 1000000000 | bytes 4000000 | tf_op jit(solution)/shard_map/pallas_call | solution.py:348
  89.6 1.3 %copy.17 = bf16[4,1024]{1,0:T(4,128)(2,1)} copy(bf16[4,1024]{1,0:T(4,128)(2,1)} %shard_map.127) | data formatting | bytes 16384

commit v3 on v2

--- a/solution.py
+++ b/solution.py
@@ -53,7 +53,7 @@
     q, kt, vup, wo, res, wg, wu, wd,
     asend, arecv, zs, zr, vbuf, ob, orz, st, agb, gs, gr, hb,
     ds_, drx, dz, drz,
-    lsem, ssem, rsem, fsem,
+    lsem, ssem, rsem, vsem, fsem,
 ):
     grp, seq, hid = lax.axis_index("grp"), lax.axis_index("seq"), lax.axis_index("hid")
     x, z = hid // 8, grp * 8 + hid % 8
@@ -96,6 +96,14 @@
         return pl.ds(pl.multiple_of(i * n, n), n)
 
     own_cols = rows(x, 256)
+    barrier = pltpu.get_barrier_semaphore()
+
+    def greet(p, device):
+        pl.semaphore_signal(barrier, inc=1, device_id=device, device_id_type=MESH)
+
+    z_peers(greet)
+    xs_peers(greet)
+
     loads = [
         pltpu.make_async_copy(a, b, lsem.at[i])
         for i, (a, b) in enumerate([
@@ -105,20 +113,13 @@
             (new_hbm, new_ref), (gain_hbm, gain_ref),
         ])
     ]
-    for load in loads:
-        load.start()
-
-    barrier = pltpu.get_barrier_semaphore()
-
-    def greet(p, device):
-        pl.semaphore_signal(barrier, inc=1, device_id=device, device_id_type=MESH)
-
-    xs_peers(greet)
-    z_peers(greet)
+    early = (1, 0, 9, 8, 11, 10)
+    for i in early:
+        loads[i].start()
 
     loads[8].wait()
     loads[9].wait()
-    places = (pos_ref[0] + iota((8, 128), 0)).astype(F32)
+    places = (jnp.broadcast_to(pos_ref[...], (8, 128)) + iota((8, 128), 0)).astype(F32)
     angles = places * freq_ref[...]
     cos_table, sin_table = jnp.cos(angles), jnp.sin(angles)
     loads[0].wait()
@@ -142,9 +143,12 @@
     new_rope = jnp.concatenate([fresh_rope, jnp.zeros((8, ROPE), F32)], axis=0).astype(BF)
     near = (dot_t(q_lat, new_lat) + dot_t(q_rope, new_rope)) * score_scale
     loads[1].wait()
+    for i in range(13):
+        if i not in early:
+            loads[i].start()
     loads[10].wait()
     far = (dot(q_lat, kt[:LATENT, :]) + dot(q_rope, kt[LATENT:, :])) * score_scale
-    usable = iota((256, 256), 1) + seq * 256 < len_ref[0]
+    usable = iota((256, 256), 1) + seq * 256 < jnp.broadcast_to(len_ref[...], (256, 256))
     causal = iota((256, 16), 1) + seq * 1024 <= iota((256, 16), 0) // 64
     peak = jnp.maximum(
         jnp.max(jnp.where(usable, far, -1e30), axis=1, keepdims=True),
@@ -208,15 +212,28 @@
         for i in range(NX):
             wide = jnp.concatenate([lat[64 * i + 16 * n:64 * i + 16 * n + 16] for n in range(4)], axis=1)
             vbuf[value_rows, 128 * i:128 * i + 128] = dot(wide, vup[i]).astype(BF)
-        xs_peers(lambda p, device: remote(
-            vbuf.at[value_rows], vbuf.at[value_rows], ssem.at[4], rsem.at[4], device).start())
+        other = at(x, z, y * 2 + 1 - core)
+        steps = sorted(
+            ((dx, dy) for dx in range(NX) for dy in range(4) if dx or dy),
+            key=lambda d: min(d[0], 4 - d[0]) + min(d[1], 4 - d[1]),
+        )
+        for dx, dy in steps[::-1]:
+            remote(
+                vbuf.at[value_rows], vbuf.at[value_rows], ssem.at[4], vsem.at[y],
+                at((x + dx) % 4, z, (y + dy) % 4 * 2 + core),
+            ).start()
+
+        for dt in (0, 1, 3, 2):
+            t = (y + dt) % 4
+            piece = vbuf.at[rows(t, 64)]
+            if dt == 0:
+                wait_bytes(vbuf.at[0:48], vsem.at[t])
+            else:
+                wait_bytes(piece, vsem.at[t])
+            remote(piece, piece, ssem.at[4], rsem.at[4], other).start()
 
     loads[3].wait()
     wait_bytes(wo.at[0:NX - 1], rsem.at[2])
-
-    @pl.when(grp == core)
-    def _():
-        wait_bytes(vbuf.at[0:240], rsem.at[4])
 
     @pl.when(grp != core)
     def _():
@@ -237,78 +254,83 @@
     st[...] = stream
     agb[tile, own_cols] = (stream * gain_ref[:, own_cols]).astype(BF)
     z_peers(lambda p, device: remote(
-        agb.at[tile, own_cols], agb.at[tile, own_cols], ssem.at[6], fsem.at[z], device).start())
-
-    def forward(p):
-        piece = agb.at[rows(p, 16), own_cols]
-        x_peers(lambda _, device: remote(piece, piece, ssem.at[7], rsem.at[7], device).start())
-
-    def arrived(i, carry):
-        p = (z + z_distance(NZ - i)) % NZ
-        wait_bytes(agb.at[rows(p, 16), own_cols], fsem.at[p])
-        forward(p)
-        return carry
-
-    forward(z)
-    lax.fori_loop(1, NZ, arrived, 0)
+        agb.at[tile, own_cols], agb.at[tile, own_cols], ssem.at[6], fsem.at[z // 4], device).start())
+
+    t_own, side = z // 4, z % 4 // 2
+    order = [t_own, (t_own + 3 + 2 * side) % 4, (t_own + 1 + 2 * side) % 4, (t_own + 2) % 4]
+
+    for n, t in enumerate(order):
+        piece = agb.at[rows(t, 64), own_cols]
+        if n == 0:
+            wait_bytes(orz.at[0:3], fsem.at[t])
+        else:
+            wait_bytes(piece, fsem.at[t])
+        x_peers(lambda _, device: remote(
+            piece, piece, ssem.at[7], rsem.at[16 + n // 2], device).start())
 
     inverse_gain = 1.0 / gain
-    lane = iota((256, 128), 1)
+    lane = iota((128, 128), 1)
     loads[5].wait()
     loads[6].wait()
-    wait_bytes(agb.at[0:192], rsem.at[7])
-    scaled = agb[...]
-    gs[:, 0:256] = dot(scaled, wg[...]).astype(BF)
-    gs[:, 256:512] = dot(scaled, wu[...]).astype(BF)
-    plain = scaled.astype(F32) * inverse_gain
-    squares = jnp.sum(plain * plain, axis=1, keepdims=True)
-    high = squares.astype(BF).astype(F32)
-    gs[:, 512:640] = jnp.where(lane == 0, high, squares - high).astype(BF)
-    s_peers(lambda p, device: remote(
-        gs.at[rows(p, 32)], gr.at[seq], ssem.at[8], rsem.at[8], device).start())
-    mine = rows(seq, 32)
-    gr[seq] = gs[mine]
-
-    wait_bytes(gr.at[0:NS - 1], rsem.at[8])
-    sums = sum(gr[i].astype(F32) for i in range(NS))
-    square = sums[:, 512:513] + sums[:, 513:514]
-    inverse = lax.rsqrt(square * (1.0 / D) + 1e-06)
-    gate = sums[:, 0:256] * inverse
-    up = sums[:, 256:512] * inverse
-    hb[mine] = (gate / (1.0 + jnp.exp(-gate)) * up).astype(BF)
-    s_peers(lambda p, device: remote(
-        hb.at[mine], hb.at[mine], ssem.at[9], rsem.at[9], device).start())
+    for c in range(2):
+        wait_bytes(agb.at[0:96], rsem.at[16 + c])
+        scaled = jnp.concatenate([agb[rows(t, 64)] for t in order[2 * c:2 * c + 2]], axis=0)
+        gs[c, :, 0:256] = dot(scaled, wg[...]).astype(BF)
+        gs[c, :, 256:512] = dot(scaled, wu[...]).astype(BF)
+        plain = scaled.astype(F32) * inverse_gain
+        squares = jnp.sum(plain * plain, axis=1, keepdims=True)
+        high = squares.astype(BF).astype(F32)
+        gs[c, :, 512:640] = jnp.where(lane == 0, high, squares - high).astype(BF)
+        s_peers(lambda p, device: remote(
+            gs.at[c, rows(p, 16)], gr.at[c, seq], ssem.at[8 + c], rsem.at[8 + c], device).start())
+        gr[c, seq] = gs[c, rows(seq, 16)]
+
+    mine = rows(seq, 16)
+    for c in range(2):
+        wait_bytes(gr.at[c, 0:NS - 1], rsem.at[8 + c])
+        sums = sum(gr[c, i].astype(F32) for i in range(NS))
+        square = sums[:, 512:513] + sums[:, 513:514]
+        inverse = lax.rsqrt(square * (1.0 / D) + 1e-06)
+        gate = sums[:, 0:256] * inverse
+        up = sums[:, 256:512] * inverse
+        hb[c, mine] = (gate / (1.0 + jnp.exp(-gate)) * up).astype(BF)
+        s_peers(lambda p, device: remote(
+            hb.at[c, mine], hb.at[c, mine], ssem.at[10 + c], rsem.at[10 + c], device).start())
 
     loads[7].wait()
-    perm_four = one_hot(256, 256, lambda o: (o // 2 % 8) * 32 + (o % 2) * 16 + o // 16)
-    wait_bytes(hb.at[0:224], rsem.at[9])
-    for c in range(2):
-        ds_[c] = dot(hb[128 * c:128 * c + 128], wd[...]).astype(BF).reshape(2, 64, 1024)
-
-        @pl.when(grp == c)
-        def _():
-            own = dot(hb[tile], wd[:, own_cols]) + st[...]
-            ds_[c, z // 4 % 2, rows(z % 4, 16), own_cols] = own.astype(BF)
-
+    perm_three = one_hot(256, 256, lambda o: (o % 8) * 32 + (o // 8 % 2) * 16 + o // 16)
+    for c in range(2):
+        wait_bytes(hb.at[c, 0:112], rsem.at[10 + c])
+        ds_[c] = dot(hb[c], wd[...]).astype(BF).reshape(2, 64, 1024)
+        if c == 0:
+            place = rows(z % 4, 16)
+            own = dot(hb[0, place], wd[:, own_cols]) + st[...]
+            ds_[0, 0, place, own_cols] = own.astype(BF)
         x_peers(lambda p, device: remote(
             ds_.at[c, :, pl.ds(pl.multiple_of(p * 16, 16), 16)], drx.at[c, x],
-            ssem.at[10 + c], rsem.at[10 + c], device).start())
+            ssem.at[12 + c], rsem.at[12 + c], device).start())
         drx[c, x] = ds_[c, :, pl.ds(pl.multiple_of(x * 16, 16), 16)]
 
     for c in range(2):
-        wait_bytes(drx.at[c, 0:NX - 1], rsem.at[10 + c])
+        wait_bytes(drx.at[c, 0:NX - 1], rsem.at[12 + c])
         summed = sum(drx[c, i].astype(F32) for i in range(NX)).astype(BF).reshape(32, 1024)
         stacked = jnp.concatenate([summed[:, 128 * i:128 * i + 128] for i in range(8)], axis=0)
-        dz[c] = dot(perm_four, stacked).astype(BF).reshape(NZ, 16, 128)
+        dz[c] = dot(perm_three, stacked).astype(BF).reshape(NZ, 16, 128)
         z_peers(lambda p, device: remote(
-            dz.at[c, p], drz.at[c, z], ssem.at[12 + c], rsem.at[12 + c], device).start())
+            dz.at[c, p], drz.at[c, z], ssem.at[14 + c], rsem.at[14 + c], device).start())
         drz[c, z] = dz[c, z]
 
     for c in range(2):
-        wait_bytes(drz.at[c, 0:NZ - 1], rsem.at[12 + c])
-        final = sum(drz[c, i].astype(F32) for i in range(NZ)).astype(BF)
-        for i in range(8):
-            out_ref[2 * c:2 * c + 2, 128 * i:128 * i + 128] = final[2 * i:2 * i + 2]
+        wait_bytes(drz.at[c, 0:NZ - 1], rsem.at[14 + c])
+    final = [0.0] * 4
+    for i in range(NZ):
+        turn = [i // 4, (i // 4 + 3 + 2 * (i % 4 // 2)) % 4, (i // 4 + 1 + 2 * (i % 4 // 2)) % 4, (i // 4 + 2) % 4]
+        for c in range(2):
+            part = drz[c, i].astype(F32)
+            for n in range(2):
+                final[turn[2 * c + n]] += part[8 * n:8 * n + 8]
+    for i in range(8):
+        out_ref[:, 128 * i:128 * i + 128] = jnp.concatenate([f[i:i + 1] for f in final], axis=0).astype(BF)
 
     wait_bytes(arecv.at[0:NS - 1], ssem.at[0])
     wait_bytes(vup.at[0:NX - 1], ssem.at[1])
@@ -326,11 +348,11 @@
     wait_bytes(orz.at[0:NZ - 1], ssem.at[5])
     wait_bytes(orz.at[0:NZ - 1], ssem.at[6])
     wait_bytes(agb.at[0:192], ssem.at[7])
-    wait_bytes(gr.at[0:NS - 1], ssem.at[8])
-    wait_bytes(hb.at[0:224], ssem.at[9])
-    for c in range(2):
-        wait_bytes(drx.at[c, 0:NX - 1], ssem.at[10 + c])
-        wait_bytes(drz.at[c, 0:NZ - 1], ssem.at[12 + c])
+    for c in range(2):
+        wait_bytes(gr.at[c, 0:NS - 1], ssem.at[8 + c])
+        wait_bytes(hb.at[c, 0:112], ssem.at[10 + c])
+        wait_bytes(drx.at[c, 0:NX - 1], ssem.at[12 + c])
+        wait_bytes(drz.at[c, 0:NZ - 1], ssem.at[14 + c])
 
 
 def body(
@@ -347,29 +369,30 @@
 
     return pl.pallas_call(
         kernel,
-        out_shape=jax.ShapeDtypeStruct((4, 1024), BF),
+        out_shape=pltpu.VMEM((4, 1024), BF),
         in_specs=[hbm] * 13,
         out_specs=vmem,
         scratch_shapes=[
-            buf(1, 128, dtype=F32), pltpu.SMEM((1,), jnp.int32), pltpu.SMEM((1,), jnp.int32),
+            buf(1, 128, dtype=F32), buf(1, 1, dtype=jnp.int32), buf(1, 1, dtype=jnp.int32),
             buf(4, 576), buf(1, 1024, dtype=F32),
             buf(256, 576), buf(576, 256), buf(NX, 512, 128), buf(NX, 128, 256), buf(256, 1024),
             buf(1024, 256), buf(1024, 256), buf(256, 1024),
             buf(256, 640), buf(NS, 32, 640), buf(8, 16, 128), buf(NZ, 16, 128),
             buf(256, 512), buf(256, 256), buf(NZ, 16, 256), buf(16, 256, dtype=F32), buf(256, 1024),
-            buf(256, 640), buf(NS, 32, 640), buf(256, 256),
+            buf(2, 128, 640), buf(2, NS, 16, 640), buf(2, 128, 256),
             buf(2, 2, 64, 1024), buf(2, NX, 2, 16, 1024), buf(2, NZ, 16, 128), buf(2, NZ, 16, 128),
             pltpu.SemaphoreType.DMA((13,)),
-            pltpu.SemaphoreType.DMA((14,)),
-            pltpu.SemaphoreType.DMA((14,)),
-            pltpu.SemaphoreType.DMA((NZ,)),
+            pltpu.SemaphoreType.DMA((16,)),
+            pltpu.SemaphoreType.DMA((18,)),
+            pltpu.SemaphoreType.DMA((4,)),
+            pltpu.SemaphoreType.DMA((4,)),
         ],
         compiler_params=pltpu.CompilerParams(
             collective_id=0, has_side_effects=True, vmem_limit_bytes=56 * 1024 * 1024,
         ),
         cost_estimate=pl.CostEstimate(flops=10**9, bytes_accessed=4 * 10**6, transcendentals=10**5),
     )(
-        frequency, positions, lengths, new_latents.reshape(4, 576), norm_gain.reshape(1, -1),
+        frequency, positions.reshape(1, 1), lengths.reshape(1, 1), new_latents.reshape(4, 576), norm_gain.reshape(1, -1),
         queries.reshape(256, 576), jnp.swapaxes(latent_cache.reshape(256, 576), 0, 1), value_up.reshape(512, 128),
         output_weight, residual, gate_weight, up_weight, down_weight,
     )

time: 91.1 us -> 84.9 us (0.932)
  Pallas kernels: 88.3 us -> 82.8 us
    pallas_call x1, Pallas kernels: 88.3 us -> 82.8 us  [body(): pl.pallas_call(kernel, out_shape=pltpu.VMEM((4, 1024), BF), in_specs=[hbm...]
where the time goes in v3:
time: 84.9 us; the launch traced here: 84.7 us
  Pallas kernels  82.8 us (98%)
  between operations  1.3 us (2%)
    pallas_call x1, Pallas kernels, body(): pl.pallas_call(kernel, out_shape=pltpu.VMEM((4, 1024), BF), in_specs=[hbm...  82.8 us

profile of v3, /device:TPU:1, one launch (start us, length us, event | category | flops | bytes accessed | tf_op | source)
XLA Modules:
  0.0 84.7 jit_solution(14965734870172781671)
XLA Ops:
  1.3 82.8 %shard_map.127 = bf16[4,1024]{1,0:T(4,128)(2,1)S(1)} custom-call(f32[1,128]{1,0:T(1,128)} %constant.2.clone.freq_hbm, s32[1,1]{1,0:T(1,128)} %bitcast.10.pos_hbm, s32[1,1]{1,0:T(1,128)} %bitcast.9.len_hbm, bf16[4,576]{1,0:T(4,128)(2,1)} %bitcast.14, f32[1,1024]{1,0:T(1,128)} %bitcast.15, bf16[256,576]{1,0:T(8,128)(2,1)} %bitcast.11, ...), custom_call_target="tpu_custom_call" | custom-call | flops 1000000000 | bytes 4000000 | tf_op jit(solution)/shard_map/pallas_call | solution.py:370
  84.1 0.6 copy.15

commit v4 on v3

--- a/solution.py
+++ b/solution.py
@@ -51,9 +51,8 @@
     out_ref,
     freq_ref, pos_ref, len_ref, new_ref, gain_ref,
     q, kt, vup, wo, res, wg, wu, wd,
-    asend, arecv, zs, zr, vbuf, ob, orz, st, agb, gs, gr, hb,
-    ds_, drx, dz, drz,
-    lsem, ssem, rsem, vsem, fsem,
+    asend, arecv, zs, zr, vbuf, ob, orz, st, agb, gs, gr, hb, ds_, drx, dz, drz,
+    lsem, ssem, rsem, fsem,
 ):
     grp, seq, hid = lax.axis_index("grp"), lax.axis_index("seq"), lax.axis_index("hid")
     x, z = hid // 8, grp * 8 + hid % 8
@@ -95,19 +94,11 @@
     def rows(i, n):
         return pl.ds(pl.multiple_of(i * n, n), n)
 
-    own_cols = rows(x, 256)
-    barrier = pltpu.get_barrier_semaphore()
-
-    def greet(p, device):
-        pl.semaphore_signal(barrier, inc=1, device_id=device, device_id_type=MESH)
-
-    z_peers(greet)
-    xs_peers(greet)
-
+    tile_r, tile_c = rows(z // 4 * 4 + x, 16), rows(z % 4, 256)
     loads = [
         pltpu.make_async_copy(a, b, lsem.at[i])
         for i, (a, b) in enumerate([
-            (q_hbm, q), (k_hbm, kt), (vup_hbm, vup.at[x]), (wo_hbm.at[:, own_cols], wo.at[x]), (res_hbm, res),
+            (q_hbm, q), (k_hbm, kt), (vup_hbm, vup.at[x]), (wo_hbm, wo.at[x]), (res_hbm, res),
             (wg_hbm, wg), (wu_hbm, wu), (wd_hbm, wd),
             (freq_hbm, freq_ref), (pos_hbm, pos_ref), (len_hbm, len_ref),
             (new_hbm, new_ref), (gain_hbm, gain_ref),
@@ -116,6 +107,14 @@
     early = (1, 0, 9, 8, 11, 10)
     for i in early:
         loads[i].start()
+
+    barrier = pltpu.get_barrier_semaphore()
+
+    def greet(p, device):
+        pl.semaphore_signal(barrier, inc=1, device_id=device, device_id_type=MESH)
+
+    z_peers(greet)
+    xs_peers(greet)
 
     loads[8].wait()
     loads[9].wait()
@@ -170,10 +169,11 @@
     s_peers(lambda p, device: remote(
         asend.at[rows(p, 32)], arecv.at[seq], ssem.at[0], rsem.at[0], device).start())
 
+    half = rows(core, 256)
     x_peers(lambda p, device: remote(
-        vup_hbm, vup.at[x], ssem.at[1], rsem.at[1], device).start())
+        vup_hbm.at[half], vup.at[x, half], ssem.at[1], rsem.at[1], device).start())
     x_peers(lambda p, device: remote(
-        wo_hbm.at[:, rows(p, 256)], wo.at[x], ssem.at[2], rsem.at[2], device).start())
+        wo_hbm, wo.at[x], ssem.at[2], rsem.at[2], device).start())
 
     arecv[seq] = asend[rows(seq, 32)]
     perm_one = one_hot(128, 128, lambda o: (o % 4) * 32 + (o // 4 % 4) * 8 + o // 16)
@@ -200,9 +200,18 @@
         return carry
 
     lax.fori_loop(0, 8, to_head, 0)
+
+    other = at(x, z, y * 2 + 1 - core)
+    wait_bytes(vup.at[0:NX - 1, 0:256], rsem.at[1])
+
+    def hand_over(p, _):
+        piece = vup.at[p, half]
+        remote(piece, piece, ssem.at[16], rsem.at[18], other).start()
+
+    x_peers(hand_over)
     loads[2].wait()
-    wait_bytes(vup.at[0:NX - 1], rsem.at[1])
-    value_rows = rows(y * 4 + x, 16)
+    wait_bytes(vup.at[0:NX - 1, 0:256], rsem.at[18])
+    value_rows = rows(y, 16)
 
     @pl.when(grp == core)
     def _():
@@ -212,55 +221,41 @@
         for i in range(NX):
             wide = jnp.concatenate([lat[64 * i + 16 * n:64 * i + 16 * n + 16] for n in range(4)], axis=1)
             vbuf[value_rows, 128 * i:128 * i + 128] = dot(wide, vup[i]).astype(BF)
-        other = at(x, z, y * 2 + 1 - core)
-        steps = sorted(
-            ((dx, dy) for dx in range(NX) for dy in range(4) if dx or dy),
-            key=lambda d: min(d[0], 4 - d[0]) + min(d[1], 4 - d[1]),
-        )
-        for dx, dy in steps[::-1]:
-            remote(
-                vbuf.at[value_rows], vbuf.at[value_rows], ssem.at[4], vsem.at[y],
-                at((x + dx) % 4, z, (y + dy) % 4 * 2 + core),
-            ).start()
-
-        for dt in (0, 1, 3, 2):
-            t = (y + dt) % 4
-            piece = vbuf.at[rows(t, 64)]
-            if dt == 0:
-                wait_bytes(vbuf.at[0:48], vsem.at[t])
-            else:
-                wait_bytes(piece, vsem.at[t])
-            remote(piece, piece, ssem.at[4], rsem.at[4], other).start()
+        s_peers(lambda p, device: remote(
+            vbuf.at[value_rows], vbuf.at[value_rows], ssem.at[4], rsem.at[4], device).start())
 
     loads[3].wait()
     wait_bytes(wo.at[0:NX - 1], rsem.at[2])
+
+    @pl.when(grp == core)
+    def _():
+        wait_bytes(vbuf.at[0:48], rsem.at[4])
 
     @pl.when(grp != core)
     def _():
         wait_bytes(vbuf, rsem.at[4])
 
-    ob[...] = dot(vbuf[...], wo[...].reshape(512, 256)).astype(BF)
+    ob[...] = dot(vbuf[...], wo[...].reshape(512, 1024)).astype(BF)
     z_peers(lambda p, device: remote(
-        ob.at[rows(p, 16)], orz.at[z], ssem.at[5], rsem.at[5], device).start())
-    tile = rows(z, 16)
-    orz[z] = ob[tile]
+        ob.at[rows(p // 4, 16), rows(p % 4, 256)], orz.at[z], ssem.at[5], rsem.at[5], device).start())
+    orz[z] = ob[rows(z // 4, 16), tile_c]
     loads[4].wait()
     loads[12].wait()
     gain = gain_ref[...]
-    own = one_hot(16, 256, lambda o: ((o // 8) * 32 + (z % 4) * 8 + o % 8) * 4 + z // 4)
-    old = dot(own, res[:, own_cols])
+    own = one_hot(16, 256, lambda o: ((o // 8) * 32 + x * 8 + o % 8) * 4 + z // 4)
+    old = dot(own, res[:, tile_c])
     wait_bytes(orz.at[0:NZ - 1], rsem.at[5])
     stream = old + sum(orz[i].astype(F32) for i in range(NZ))
     st[...] = stream
-    agb[tile, own_cols] = (stream * gain_ref[:, own_cols]).astype(BF)
+    agb[tile_r, tile_c] = (stream * gain_ref[:, tile_c]).astype(BF)
     z_peers(lambda p, device: remote(
-        agb.at[tile, own_cols], agb.at[tile, own_cols], ssem.at[6], fsem.at[z // 4], device).start())
+        agb.at[tile_r, tile_c], agb.at[tile_r, tile_c], ssem.at[6], fsem.at[z // 4], device).start())
 
     t_own, side = z // 4, z % 4 // 2
     order = [t_own, (t_own + 3 + 2 * side) % 4, (t_own + 1 + 2 * side) % 4, (t_own + 2) % 4]
 
     for n, t in enumerate(order):
-        piece = agb.at[rows(t, 64), own_cols]
+        piece = agb.at[rows(t * 4 + x, 16)]
         if n == 0:
             wait_bytes(orz.at[0:3], fsem.at[t])
         else:
@@ -303,9 +298,9 @@
         wait_bytes(hb.at[c, 0:112], rsem.at[10 + c])
         ds_[c] = dot(hb[c], wd[...]).astype(BF).reshape(2, 64, 1024)
         if c == 0:
-            place = rows(z % 4, 16)
-            own = dot(hb[0, place], wd[:, own_cols]) + st[...]
-            ds_[0, 0, place, own_cols] = own.astype(BF)
+            place = rows(x, 16)
+            own = dot(hb[0, place], wd[:, tile_c]) + st[...]
+            ds_[0, 0, place, tile_c] = own.astype(BF)
         x_peers(lambda p, device: remote(
             ds_.at[c, :, pl.ds(pl.multiple_of(p * 16, 16), 16)], drx.at[c, x],
             ssem.at[12 + c], rsem.at[12 + c], device).start())
@@ -333,13 +328,14 @@
         out_ref[:, 128 * i:128 * i + 128] = jnp.concatenate([f[i:i + 1] for f in final], axis=0).astype(BF)
 
     wait_bytes(arecv.at[0:NS - 1], ssem.at[0])
-    wait_bytes(vup.at[0:NX - 1], ssem.at[1])
+    wait_bytes(vup.at[0:NX - 1, 0:256], ssem.at[1])
+    wait_bytes(vup.at[0:NX - 1, 0:256], ssem.at[16])
     wait_bytes(wo.at[0:NX - 1], ssem.at[2])
 
     @pl.when(grp == core)
     def _():
         wait_bytes(zs.at[0:7], ssem.at[3])
-        wait_bytes(wg.at[0:992], ssem.at[4])
+        wait_bytes(wg.at[0:224], ssem.at[4])
 
     @pl.when(grp != core)
     def _():
@@ -375,16 +371,15 @@
         scratch_shapes=[
             buf(1, 128, dtype=F32), buf(1, 1, dtype=jnp.int32), buf(1, 1, dtype=jnp.int32),
             buf(4, 576), buf(1, 1024, dtype=F32),
-            buf(256, 576), buf(576, 256), buf(NX, 512, 128), buf(NX, 128, 256), buf(256, 1024),
+            buf(256, 576), buf(576, 256), buf(NX, 512, 128), buf(NX, 128, 1024), buf(256, 1024),
             buf(1024, 256), buf(1024, 256), buf(256, 1024),
             buf(256, 640), buf(NS, 32, 640), buf(8, 16, 128), buf(NZ, 16, 128),
-            buf(256, 512), buf(256, 256), buf(NZ, 16, 256), buf(16, 256, dtype=F32), buf(256, 1024),
+            buf(64, 512), buf(64, 1024), buf(NZ, 16, 256), buf(16, 256, dtype=F32), buf(256, 1024),
             buf(2, 128, 640), buf(2, NS, 16, 640), buf(2, 128, 256),
             buf(2, 2, 64, 1024), buf(2, NX, 2, 16, 1024), buf(2, NZ, 16, 128), buf(2, NZ, 16, 128),
             pltpu.SemaphoreType.DMA((13,)),
-            pltpu.SemaphoreType.DMA((16,)),
-            pltpu.SemaphoreType.DMA((18,)),
-            pltpu.SemaphoreType.DMA((4,)),
+            pltpu.SemaphoreType.DMA((17,)),
+            pltpu.SemaphoreType.DMA((19,)),
             pltpu.SemaphoreType.DMA((4,)),
         ],
         compiler_params=pltpu.CompilerParams(

time: 84.9 us -> 82 us (0.966)
  Pallas kernels: 82.8 us -> 79.8 us
    pallas_call x1, Pallas kernels: 82.8 us -> 79.8 us  [body(): pl.pallas_call(kernel, out_shape=pltpu.VMEM((4, 1024), BF), in_specs=[hbm...]
where the time goes in v4:
time: 82 us; the launch traced here: 81.7 us
  Pallas kernels  79.8 us (97%)
  between operations  1.3 us (2%)
    pallas_call x1, Pallas kernels, body(): pl.pallas_call(kernel, out_shape=pltpu.VMEM((4, 1024), BF), in_specs=[hbm...  79.8 us

profile of v4, /device:TPU:1, one launch (start us, length us, event | category | flops | bytes accessed | tf_op | source)
XLA Modules:
  0.0 81.7 jit_solution(4652446016947915087)
XLA Ops:
  1.3 79.8 %shard_map.127 = bf16[4,1024]{1,0:T(4,128)(2,1)S(1)} custom-call(f32[1,128]{1,0:T(1,128)} %constant.2.clone.freq_hbm, s32[1,1]{1,0:T(1,128)} %bitcast.10.pos_hbm, s32[1,1]{1,0:T(1,128)} %bitcast.9.len_hbm, bf16[4,576]{1,0:T(4,128)(2,1)} %bitcast.14, f32[1,1024]{1,0:T(1,128)} %bitcast.15, bf16[256,576]{1,0:T(8,128)(2,1)} %bitcast.11, ...), custom_call_target="tpu_custom_call" | custom-call | flops 1000000000 | bytes 4000000 | tf_op jit(solution)/shard_map/pallas_call | solution.py:366
  81.1 0.6 copy.15

commit v5 on v4

--- a/solution.py
+++ b/solution.py
@@ -51,7 +51,7 @@
     out_ref,
     freq_ref, pos_ref, len_ref, new_ref, gain_ref,
     q, kt, vup, wo, res, wg, wu, wd,
-    asend, arecv, zs, zr, vbuf, ob, orz, st, agb, gs, gr, hb, ds_, drx, dz, drz,
+    asend, arecv, zs, zr, vbuf, ob, orz, st, agb, gs, gr, hs, hb, ds_, dz, drz,
     lsem, ssem, rsem, fsem,
 ):
     grp, seq, hid = lax.axis_index("grp"), lax.axis_index("seq"), lax.axis_index("hid")
@@ -61,9 +61,12 @@
     def at(xx, zz, ss):
         return (zz // 8, ss, xx * 8 + zz % 8)
 
+    def distance(count, i):
+        return count // 2 + (1 - 2 * (i % 2)) * (i // 2)
+
     def each(count, me, fn):
         def step(i, carry):
-            fn((me + i) % count)
+            fn((me + distance(count, i)) % count)
             return carry
         lax.fori_loop(1, count, step, 0)
 
@@ -73,15 +76,8 @@
     def s_peers(fn):
         each(NS, seq, lambda p: fn(p, at(x, z, p)))
 
-    def z_distance(i):
-        return 8 + (1 - 2 * (i % 2)) * (i // 2)
-
     def z_peers(fn):
-        def step(i, carry):
-            p = (z + z_distance(i)) % NZ
-            fn(p, at(x, p, seq))
-            return carry
-        lax.fori_loop(1, NZ, step, 0)
+        each(NZ, z, lambda p: fn(p, at(x, p, seq)))
 
     def xs_peers(fn):
         for dx in (2, 1, 3, 0):
@@ -99,7 +95,7 @@
         pltpu.make_async_copy(a, b, lsem.at[i])
         for i, (a, b) in enumerate([
             (q_hbm, q), (k_hbm, kt), (vup_hbm, vup.at[x]), (wo_hbm, wo.at[x]), (res_hbm, res),
-            (wg_hbm, wg), (wu_hbm, wu), (wd_hbm, wd),
+            (wg_hbm, wg), (wu_hbm, wu), (wd_hbm, wd.at[x]),
             (freq_hbm, freq_ref), (pos_hbm, pos_ref), (len_hbm, len_ref),
             (new_hbm, new_ref), (gain_hbm, gain_ref),
         ])
@@ -201,6 +197,10 @@
 
     lax.fori_loop(0, 8, to_head, 0)
 
+    left, right = (x + 3) % NX, (x + 1) % NX
+    for p, sem in ((right, 12), (left, 19)):
+        remote(wd_hbm, wd.at[x], ssem.at[12], rsem.at[sem], at(p, z, seq)).start()
+
     other = at(x, z, y * 2 + 1 - core)
     wait_bytes(vup.at[0:NX - 1, 0:256], rsem.at[1])
 
@@ -239,6 +239,10 @@
     z_peers(lambda p, device: remote(
         ob.at[rows(p // 4, 16), rows(p % 4, 256)], orz.at[z], ssem.at[5], rsem.at[5], device).start())
     orz[z] = ob[rows(z // 4, 16), tile_c]
+    for p, sem, to, part in ((left, 12, right, 0), (right, 19, left, 1)):
+        wait_bytes(wd.at[p], rsem.at[sem])
+        piece = wd.at[p, 128 * part:128 * part + 128]
+        remote(piece, piece, ssem.at[12], rsem.at[20], at(to, z, seq)).start()
     loads[4].wait()
     loads[12].wait()
     gain = gain_ref[...]
@@ -280,7 +284,7 @@
             gs.at[c, rows(p, 16)], gr.at[c, seq], ssem.at[8 + c], rsem.at[8 + c], device).start())
         gr[c, seq] = gs[c, rows(seq, 16)]
 
-    mine = rows(seq, 16)
+    seq_x, seq_t = seq % 4, seq // 4
     for c in range(2):
         wait_bytes(gr.at[c, 0:NS - 1], rsem.at[8 + c])
         sums = sum(gr[c, i].astype(F32) for i in range(NS))
@@ -288,42 +292,49 @@
         inverse = lax.rsqrt(square * (1.0 / D) + 1e-06)
         gate = sums[:, 0:256] * inverse
         up = sums[:, 256:512] * inverse
-        hb[c, mine] = (gate / (1.0 + jnp.exp(-gate)) * up).astype(BF)
-        s_peers(lambda p, device: remote(
-            hb.at[c, mine], hb.at[c, mine], ssem.at[10 + c], rsem.at[10 + c], device).start())
-
+        hs[c] = (gate / (1.0 + jnp.exp(-gate)) * up).astype(BF)
+
+        def to_x(p, device):
+            place = hb.at[c, rows(seq_t, 16), rows(x, 256)]
+            remote(hs.at[c], place, ssem.at[10 + c], rsem.at[10 + c], at(seq_x, z, p)).start()
+
+        s_peers(to_x)
+
+        @pl.when(seq_x != x)
+        def _():
+            to_x(seq, None)
+
+        @pl.when(seq_x == x)
+        def _():
+            hb[c, rows(seq_t, 16), rows(x, 256)] = hs[c]
+
+    perm_three = one_hot(512, 512, lambda o: (o % 8) * 64 + (o // 8 % 4) * 16 + o // 32)
     loads[7].wait()
-    perm_three = one_hot(256, 256, lambda o: (o % 8) * 32 + (o // 8 % 2) * 16 + o // 16)
+    wait_bytes(wd.at[0], rsem.at[20])
     for c in range(2):
-        wait_bytes(hb.at[c, 0:112], rsem.at[10 + c])
-        ds_[c] = dot(hb[c], wd[...]).astype(BF).reshape(2, 64, 1024)
-        if c == 0:
-            place = rows(x, 16)
-            own = dot(hb[0, place], wd[:, tile_c]) + st[...]
-            ds_[0, 0, place, tile_c] = own.astype(BF)
-        x_peers(lambda p, device: remote(
-            ds_.at[c, :, pl.ds(pl.multiple_of(p * 16, 16), 16)], drx.at[c, x],
-            ssem.at[12 + c], rsem.at[12 + c], device).start())
-        drx[c, x] = ds_[c, :, pl.ds(pl.multiple_of(x * 16, 16), 16)]
-
-    for c in range(2):
-        wait_bytes(drx.at[c, 0:NX - 1], rsem.at[12 + c])
-        summed = sum(drx[c, i].astype(F32) for i in range(NX)).astype(BF).reshape(32, 1024)
-        stacked = jnp.concatenate([summed[:, 128 * i:128 * i + 128] for i in range(8)], axis=0)
-        dz[c] = dot(perm_three, stacked).astype(BF).reshape(NZ, 16, 128)
-        z_peers(lambda p, device: remote(
-            dz.at[c, p], drz.at[c, z], ssem.at[14 + c], rsem.at[14 + c], device).start())
-        drz[c, z] = dz[c, z]
-
-    for c in range(2):
-        wait_bytes(drz.at[c, 0:NZ - 1], rsem.at[14 + c])
+        @pl.when(seq_x == x)
+        def _():
+            wait_bytes(wg.at[0:112], rsem.at[10 + c])
+
+        @pl.when(seq_x != x)
+        def _():
+            wait_bytes(wg.at[0:128], rsem.at[10 + c])
+
+    ds_[...] = dot(hb[...].reshape(64, 1024), wd[...].reshape(1024, 1024))
+    ds_[0:16, tile_c] = ds_[0:16, tile_c] + st[...]
+    stacked = jnp.concatenate([ds_[:, 128 * i:128 * i + 128].astype(BF) for i in range(8)], axis=0)
+    dz[...] = dot(perm_three, stacked).astype(BF).reshape(NZ, 32, 128)
+    z_peers(lambda p, device: remote(
+        dz.at[p], drz.at[z], ssem.at[13], rsem.at[13], device).start())
+    drz[z] = dz[z]
+    wait_bytes(drz.at[0:NZ - 1], rsem.at[13])
     final = [0.0] * 4
     for i in range(NZ):
-        turn = [i // 4, (i // 4 + 3 + 2 * (i % 4 // 2)) % 4, (i // 4 + 1 + 2 * (i % 4 // 2)) % 4, (i // 4 + 2) % 4]
-        for c in range(2):
-            part = drz[c, i].astype(F32)
-            for n in range(2):
-                final[turn[2 * c + n]] += part[8 * n:8 * n + 8]
+        t, side = i // 4, i % 4 // 2
+        turn = [t, (t + 3 + 2 * side) % 4, (t + 1 + 2 * side) % 4, (t + 2) % 4]
+        part = drz[i].astype(F32)
+        for n in range(4):
+            final[turn[n]] += part[8 * n:8 * n + 8]
     for i in range(8):
         out_ref[:, 128 * i:128 * i + 128] = jnp.concatenate([f[i:i + 1] for f in final], axis=0).astype(BF)
 
@@ -346,9 +357,17 @@
     wait_bytes(agb.at[0:192], ssem.at[7])
     for c in range(2):
         wait_bytes(gr.at[c, 0:NS - 1], ssem.at[8 + c])
-        wait_bytes(hb.at[c, 0:112], ssem.at[10 + c])
-        wait_bytes(drx.at[c, 0:NX - 1], ssem.at[12 + c])
-        wait_bytes(drz.at[c, 0:NZ - 1], ssem.at[14 + c])
+
+        @pl.when(seq_x == x)
+        def _():
+            wait_bytes(wg.at[0:112], ssem.at[10 + c])
+
+        @pl.when(seq_x != x)
+        def _():
+            wait_bytes(wg.at[0:128], ssem.at[10 + c])
+
+    wait_bytes(wd.at[0:NX - 1], ssem.at[12])
+    wait_bytes(drz.at[0:NZ - 1], ssem.at[13])
 
 
 def body(
@@ -372,14 +391,14 @@
             buf(1, 128, dtype=F32), buf(1, 1, dtype=jnp.int32), buf(1, 1, dtype=jnp.int32),
             buf(4, 576), buf(1, 1024, dtype=F32),
             buf(256, 576), buf(576, 256), buf(NX, 512, 128), buf(NX, 128, 1024), buf(256, 1024),
-            buf(1024, 256), buf(1024, 256), buf(256, 1024),
+            buf(1024, 256), buf(1024, 256), buf(NX, 256, 1024),
             buf(256, 640), buf(NS, 32, 640), buf(8, 16, 128), buf(NZ, 16, 128),
             buf(64, 512), buf(64, 1024), buf(NZ, 16, 256), buf(16, 256, dtype=F32), buf(256, 1024),
-            buf(2, 128, 640), buf(2, NS, 16, 640), buf(2, 128, 256),
-            buf(2, 2, 64, 1024), buf(2, NX, 2, 16, 1024), buf(2, NZ, 16, 128), buf(2, NZ, 16, 128),
+            buf(2, 128, 640), buf(2, NS, 16, 640), buf(2, 16, 256), buf(2, 32, 1024),
+            buf(64, 1024, dtype=F32), buf(NZ, 32, 128), buf(NZ, 32, 128),
             pltpu.SemaphoreType.DMA((13,)),
             pltpu.SemaphoreType.DMA((17,)),
-            pltpu.SemaphoreType.DMA((19,)),
+            pltpu.SemaphoreType.DMA((21,)),
             pltpu.SemaphoreType.DMA((4,)),
         ],
         compiler_params=pltpu.CompilerParams(

time: 82 us -> 81 us (0.988)
  Pallas kernels: 79.8 us -> 78.9 us
    pallas_call x1, Pallas kernels: 79.8 us -> 78.9 us  [body(): pl.pallas_call(kernel, out_shape=pltpu.VMEM((4, 1024), BF), in_specs=[hbm...]
where the time goes in v5:
time: 81 us; the launch traced here: 80.8 us
  Pallas kernels  78.9 us (97%)
  between operations  1.3 us (2%)
    pallas_call x1, Pallas kernels, body(): pl.pallas_call(kernel, out_shape=pltpu.VMEM((4, 1024), BF), in_specs=[hbm...  78.9 us

profile of v5, /device:TPU:1, one launch (start us, length us, event | category | flops | bytes accessed | tf_op | source)
XLA Modules:
  0.0 80.8 jit_solution(3579263188804536045)
XLA Ops:
  1.3 78.9 %shard_map.127 = bf16[4,1024]{1,0:T(4,128)(2,1)S(1)} custom-call(f32[1,128]{1,0:T(1,128)} %constant.2.clone.freq_hbm, s32[1,1]{1,0:T(1,128)} %bitcast.10.pos_hbm, s32[1,1]{1,0:T(1,128)} %bitcast.9.len_hbm, bf16[4,576]{1,0:T(4,128)(2,1)} %bitcast.14, f32[1,1024]{1,0:T(1,128)} %bitcast.15, bf16[256,576]{1,0:T(8,128)(2,1)} %bitcast.11, ...), custom_call_target="tpu_custom_call" | custom-call | flops 1000000000 | bytes 4000000 | tf_op jit(solution)/shard_map/pallas_call | solution.py:385
  80.2 0.6 copy.15

commit v6 on v5

--- a/solution.py
+++ b/solution.py
@@ -239,10 +239,6 @@
     z_peers(lambda p, device: remote(
         ob.at[rows(p // 4, 16), rows(p % 4, 256)], orz.at[z], ssem.at[5], rsem.at[5], device).start())
     orz[z] = ob[rows(z // 4, 16), tile_c]
-    for p, sem, to, part in ((left, 12, right, 0), (right, 19, left, 1)):
-        wait_bytes(wd.at[p], rsem.at[sem])
-        piece = wd.at[p, 128 * part:128 * part + 128]
-        remote(piece, piece, ssem.at[12], rsem.at[20], at(to, z, seq)).start()
     loads[4].wait()
     loads[12].wait()
     gain = gain_ref[...]
@@ -254,6 +250,11 @@
     agb[tile_r, tile_c] = (stream * gain_ref[:, tile_c]).astype(BF)
     z_peers(lambda p, device: remote(
         agb.at[tile_r, tile_c], agb.at[tile_r, tile_c], ssem.at[6], fsem.at[z // 4], device).start())
+
+    for p, sem, to, part in ((left, 12, right, 0), (right, 19, left, 1)):
+        wait_bytes(wd.at[p], rsem.at[sem])
+        piece = wd.at[p, 128 * part:128 * part + 128]
+        remote(piece, piece, ssem.at[12], rsem.at[20], at(to, z, seq)).start()
 
     t_own, side = z // 4, z % 4 // 2
     order = [t_own, (t_own + 3 + 2 * side) % 4, (t_own + 1 + 2 * side) % 4, (t_own + 2) % 4]

time: 81 us -> 78.6 us (0.970)
  Pallas kernels: 78.9 us -> 76.3 us
    pallas_call x1, Pallas kernels: 78.9 us -> 76.3 us  [body(): pl.pallas_call(kernel, out_shape=pltpu.VMEM((4, 1024), BF), in_specs=[hbm...]
where the time goes in v6:
time: 78.6 us; the launch traced here: 78.2 us
  Pallas kernels  76.3 us (97%)
  between operations  1.3 us (2%)
    pallas_call x1, Pallas kernels, body(): pl.pallas_call(kernel, out_shape=pltpu.VMEM((4, 1024), BF), in_specs=[hbm...  76.3 us

profile of v6, /device:TPU:1, one launch (start us, length us, event | category | flops | bytes accessed | tf_op | source)
XLA Modules:
  0.0 78.2 jit_solution(15903684522268152826)
XLA Ops:
  1.3 76.3 %shard_map.127 = bf16[4,1024]{1,0:T(4,128)(2,1)S(1)} custom-call(f32[1,128]{1,0:T(1,128)} %constant.2.clone.freq_hbm, s32[1,1]{1,0:T(1,128)} %bitcast.10.pos_hbm, s32[1,1]{1,0:T(1,128)} %bitcast.9.len_hbm, bf16[4,576]{1,0:T(4,128)(2,1)} %bitcast.14, f32[1,1024]{1,0:T(1,128)} %bitcast.15, bf16[256,576]{1,0:T(8,128)(2,1)} %bitcast.11, ...), custom_call_target="tpu_custom_call" | custom-call | flops 1000000000 | bytes 4000000 | tf_op jit(solution)/shard_map/pallas_call | solution.py:386
  77.6 0.6 copy.15

commit v7 on v6

--- a/solution.py
+++ b/solution.py
@@ -251,11 +251,6 @@
     z_peers(lambda p, device: remote(
         agb.at[tile_r, tile_c], agb.at[tile_r, tile_c], ssem.at[6], fsem.at[z // 4], device).start())
 
-    for p, sem, to, part in ((left, 12, right, 0), (right, 19, left, 1)):
-        wait_bytes(wd.at[p], rsem.at[sem])
-        piece = wd.at[p, 128 * part:128 * part + 128]
-        remote(piece, piece, ssem.at[12], rsem.at[20], at(to, z, seq)).start()
-
     t_own, side = z // 4, z % 4 // 2
     order = [t_own, (t_own + 3 + 2 * side) % 4, (t_own + 1 + 2 * side) % 4, (t_own + 2) % 4]
 
@@ -267,6 +262,11 @@
             wait_bytes(piece, fsem.at[t])
         x_peers(lambda _, device: remote(
             piece, piece, ssem.at[7], rsem.at[16 + n // 2], device).start())
+
+    for p, sem, to, part in ((left, 12, right, 0), (right, 19, left, 1)):
+        wait_bytes(wd.at[p], rsem.at[sem])
+        piece = wd.at[p, 128 * part:128 * part + 128]
+        remote(piece, piece, ssem.at[12], rsem.at[20], at(to, z, seq)).start()
 
     inverse_gain = 1.0 / gain
     lane = iota((128, 128), 1)

time: 78.6 us -> 78.9 us (level)
  no operation moved by 1% of the time
where the time goes in v7:
time: 78.9 us; the launch traced here: 78.8 us
  Pallas kernels  76.9 us (97%)
  between operations  1.3 us (2%)
    pallas_call x1, Pallas kernels, body(): pl.pallas_call(kernel, out_shape=pltpu.VMEM((4, 1024), BF), in_specs=[hbm...  76.9 us

profile of v7, /device:TPU:1, one launch (start us, length us, event | category | flops | bytes accessed | tf_op | source)
XLA Modules:
  0.0 78.8 jit_solution(15718281265614915404)
XLA Ops:
  1.3 76.9 %shard_map.127 = bf16[4,1024]{1,0:T(4,128)(2,1)S(1)} custom-call(f32[1,128]{1,0:T(1,128)} %constant.2.clone.freq_hbm, s32[1,1]{1,0:T(1,128)} %bitcast.10.pos_hbm, s32[1,1]{1,0:T(1,128)} %bitcast.9.len_hbm, bf16[4,576]{1,0:T(4,128)(2,1)} %bitcast.14, f32[1,1024]{1,0:T(1,128)} %bitcast.15, bf16[256,576]{1,0:T(8,128)(2,1)} %bitcast.11, ...), custom_call_target="tpu_custom_call" | custom-call | flops 1000000000 | bytes 4000000 | tf_op jit(solution)/shard_map/pallas_call | solution.py:386
  78.2 0.6 copy.15
